TPU v7x, 32 devices: a whole 2x2x4 slice. The times are simulated.
32 devices in a mesh: groups: 2 (over y), heads: 4 (over z), seq: 4 (over x, core).
Axes of the slice: x: 2, y: 2, z: 4, core: 2. Of those that a mesh axis runs over, the one named last changes fastest.
Arguments:
- mixer_in: bfloat16 [4, 4096, 4096], P('groups', 'seq', 'heads'), parts along dimension 0, may hold values from -6 to 6
- cotangent: bfloat16 [4, 4096, 4096], P('groups', 'seq', 'heads'), parts along dimension 0, may hold values from -0.375 to 0.375
- b_proj: bfloat16 [4, 4096, 64], P('groups', 'seq'), parts along dimension 0, may hold values from -3 to 3
- c_proj: bfloat16 [4, 4096, 64], P('groups', 'seq'), parts along dimension 0, may hold values from -0.75 to 0.75
- log_decay: float32 [4, 64, 4096], P('groups', 'heads', 'seq'), parts along dimension 0, may hold values from -1.5 to 0
- skip_gain: float32 [64], P('heads'), may hold values from 0.25 to 1.75
- offsets: int32 [4], P('groups'), parts along dimension 0, may hold values from 0 to 3, as said below
- resets: int32 [4, 2], P('groups'), parts along dimension 0, may hold values from 1 to 4095
Outputs:
- mixed_out: bfloat16 [4, 4096, 4096], P('groups', 'seq', 'heads'), parts along dimension 0
- grad_in: bfloat16 [4, 4096, 4096], P('groups', 'seq', 'heads'), parts along dimension 0
- grad_b: float32 [4, 4096, 64], P('groups', 'seq'), parts along dimension 0
- grad_c: float32 [4, 4096, 64], P('groups', 'seq'), parts along dimension 0
There are 2 independent parts, one for each index of `groups`. A program takes and returns all parts, laid end to end along the dimension named above; an argument that names none is the same for every part. Nothing has to cross between parts.
Inputs may be any that keep to these rules, and one draw needn't show every extreme that they name: `offsets`: the sequences start on distinct devices; one starts on device 0 and one on device 4 - 1.
All inputs are finite; a program needn't handle non-finite values.
Results may differ from a plain program's by a relative error of at most 0.0056.
Values sent between devices are 32-bit elements; how exact they have to be, the bound alone decides.
A program may use at most 192 MiB of HBM per device.

v0:
```python
import jax
import jax.numpy as jnp
from jax import lax
from jax.sharding import PartitionSpec as P


def passed_along(value, axis, steps):
    count = lax.axis_size(axis)
    pairs = [(source, (source + steps) % count) for source in range(count)]
    return lax.ppermute(value, axis, pairs)


def block_local(
    inputs_head, cot_head, b_rows, c_rows, decay_row, skip_value, doc_ids, gram, prev_doc, next_doc
):
    block_len = decay_row.shape[0]
    cum_log = jnp.cumsum(decay_row)
    excl_log = cum_log - decay_row
    total_log = cum_log[block_len - 1]
    input_scale = jnp.sqrt(-jnp.expm1(2.0 * decay_row))
    same_doc = doc_ids[:, None] == doc_ids[None, :]
    row_index = lax.broadcasted_iota(jnp.int32, (block_len, block_len), 0)
    col_index = lax.broadcasted_iota(jnp.int32, (block_len, block_len), 1)
    causal = jnp.where(
        same_doc & (col_index <= row_index),
        jnp.exp(jnp.minimum(cum_log[:, None] - cum_log[None, :], 0.0)),
        0.0,
    )
    anticausal = jnp.where(
        same_doc & (col_index >= row_index),
        jnp.exp(jnp.minimum(excl_log[None, :] - excl_log[:, None], 0.0)),
        0.0,
    )
    mixing = causal + anticausal
    scaled = (input_scale[:, None] * inputs_head).astype(jnp.bfloat16)
    mixed_gram = (mixing * gram).astype(jnp.bfloat16)
    inner_prod = jnp.dot(cot_head, scaled.T, preferred_element_type=jnp.float32)
    mixed_inner = (mixing * inner_prod).astype(jnp.bfloat16)
    out_local = (
        jnp.dot(mixed_gram, scaled, preferred_element_type=jnp.float32) + skip_value * inputs_head
    )
    grad_local = (
        input_scale[:, None] * jnp.dot(mixed_gram.T, cot_head, preferred_element_type=jnp.float32)
        + skip_value * cot_head
    )
    gradb_local = jnp.dot(mixed_inner.T, c_rows, preferred_element_type=jnp.float32)
    gradc_local = jnp.dot(mixed_inner, b_rows, preferred_element_type=jnp.float32)
    last_doc = doc_ids[block_len - 1]
    first_doc = doc_ids[0]
    keep_last = (doc_ids == last_doc).astype(jnp.float32)
    keep_first = (doc_ids == first_doc).astype(jnp.float32)
    weight_h = (b_rows * (jnp.exp(total_log - cum_log) * keep_last)[:, None]).astype(jnp.bfloat16)
    weight_m = (c_rows * (jnp.exp(total_log - excl_log) * keep_last)[:, None]).astype(jnp.bfloat16)
    weight_g = (b_rows * (jnp.exp(excl_log) * keep_first)[:, None]).astype(jnp.bfloat16)
    weight_l = (c_rows * (jnp.exp(cum_log) * keep_first)[:, None]).astype(jnp.bfloat16)
    state_h = jnp.dot(weight_h.T, scaled, preferred_element_type=jnp.float32)
    state_m = jnp.dot(weight_m.T, cot_head, preferred_element_type=jnp.float32)
    state_g = jnp.dot(weight_g.T, scaled, preferred_element_type=jnp.float32)
    state_l = jnp.dot(weight_l.T, cot_head, preferred_element_type=jnp.float32)
    fwd_local = jnp.concatenate([state_h, state_m], axis=1)
    bwd_local = jnp.concatenate([state_g, state_l], axis=1)
    fwd_factor = jnp.exp(total_log) * (last_doc == prev_doc).astype(jnp.float32)
    bwd_factor = jnp.exp(total_log) * (first_doc == next_doc).astype(jnp.float32)
    prev_keep = (doc_ids == prev_doc).astype(jnp.float32)
    next_keep = (doc_ids == next_doc).astype(jnp.float32)
    coefs = jnp.stack(
        [
            jnp.exp(cum_log) * prev_keep,
            jnp.exp(excl_log) * prev_keep,
            jnp.exp(total_log - excl_log) * next_keep,
            jnp.exp(total_log - cum_log) * next_keep,
        ]
    )
    return (
        out_local,
        grad_local,
        gradb_local,
        gradc_local,
        fwd_local,
        bwd_local,
        fwd_factor,
        bwd_factor,
        coefs,
        input_scale,
        scaled,
    )


def finish(
    out_local,
    grad_local,
    gradb_local,
    gradc_local,
    coefs,
    input_scale,
    scaled,
    cot_head,
    b_rows,
    c_rows,
    fwd_in,
    bwd_in,
):
    head_dim = cot_head.shape[1]
    state_h = fwd_in[:, :head_dim].astype(jnp.bfloat16)
    state_m = fwd_in[:, head_dim:].astype(jnp.bfloat16)
    state_g = bwd_in[:, :head_dim].astype(jnp.bfloat16)
    state_l = bwd_in[:, head_dim:].astype(jnp.bfloat16)
    alpha = coefs[0][:, None]
    delta = coefs[1][:, None]
    beta = coefs[2][:, None]
    gamma = coefs[3][:, None]
    mixed = (
        out_local
        + alpha * jnp.dot(c_rows, state_h, preferred_element_type=jnp.float32)
        + beta * jnp.dot(c_rows, state_g, preferred_element_type=jnp.float32)
    )
    grad = grad_local + input_scale[:, None] * (
        gamma * jnp.dot(b_rows, state_l, preferred_element_type=jnp.float32)
        + delta * jnp.dot(b_rows, state_m, preferred_element_type=jnp.float32)
    )
    grad_bb = (
        gradb_local
        + gamma * jnp.dot(scaled, state_l.T, preferred_element_type=jnp.float32)
        + delta * jnp.dot(scaled, state_m.T, preferred_element_type=jnp.float32)
    )
    grad_cc = (
        gradc_local
        + alpha * jnp.dot(cot_head, state_h.T, preferred_element_type=jnp.float32)
        + beta * jnp.dot(cot_head, state_g.T, preferred_element_type=jnp.float32)
    )
    return (mixed.astype(jnp.bfloat16), grad.astype(jnp.bfloat16), grad_bb, grad_cc)


def per_device(mixer_in, cotangent, b_proj, c_proj, log_decay, skip_gain, offsets, resets):
    seq_count, block_len, row_width = mixer_in.shape
    heads_here = log_decay.shape[1]
    head_dim = row_width // heads_here
    cycle_len = lax.axis_size("seq")
    cycle_place = lax.axis_index("seq")
    local_parts = []
    cot_parts = []
    first_flags = []
    last_flags = []
    for seq_id in range(seq_count):
        block_id = jnp.mod(cycle_place - offsets[seq_id], cycle_len)
        block_start = block_id * block_len
        token_offset = block_start + jnp.arange(block_len, dtype=jnp.int32)
        bounds = resets[seq_id]
        doc_ids = jnp.sum((token_offset[:, None] >= bounds[None, :]).astype(jnp.int32), axis=1)
        prev_doc = jnp.sum((block_start - 1 >= bounds).astype(jnp.int32))
        next_doc = jnp.sum((block_start + block_len >= bounds).astype(jnp.int32))
        b_rows = b_proj[seq_id]
        c_rows = c_proj[seq_id]
        gram = jnp.dot(c_rows, b_rows.T, preferred_element_type=jnp.float32)
        inputs_heads = mixer_in[seq_id].reshape(block_len, heads_here, head_dim).transpose(1, 0, 2)
        cot_heads = cotangent[seq_id].reshape(block_len, heads_here, head_dim).transpose(1, 0, 2)

        def per_head(element):
            return block_local(
                element[0],
                element[1],
                b_rows,
                c_rows,
                element[2],
                element[3],
                doc_ids,
                gram,
                prev_doc,
                next_doc,
            )

        local_parts.append(
            lax.map(per_head, (inputs_heads, cot_heads, log_decay[seq_id], skip_gain))
        )
        cot_parts.append(cot_heads)
        first_flags.append((block_id != 0).astype(jnp.float32))
        last_flags.append((block_id != cycle_len - 1).astype(jnp.float32))
    fwd_local = jnp.stack([piece[4] for piece in local_parts])
    bwd_local = jnp.stack([piece[5] for piece in local_parts])
    fwd_factor = jnp.stack([piece[6] for piece in local_parts])
    bwd_factor = jnp.stack([piece[7] for piece in local_parts])
    not_first = jnp.stack(first_flags)[:, None]
    not_last = jnp.stack(last_flags)[:, None]

    def relay(step_index, carried):
        fwd_carry, bwd_carry = carried
        fwd_out = fwd_factor[:, :, None, None] * fwd_carry + fwd_local
        bwd_out = bwd_factor[:, :, None, None] * bwd_carry + bwd_local
        fwd_next = passed_along(fwd_out, "seq", 1) * not_first[:, :, None, None]
        bwd_next = passed_along(bwd_out, "seq", -1) * not_last[:, :, None, None]
        return (fwd_next, bwd_next)

    zero_state = jnp.zeros(fwd_local.shape, jnp.float32)
    fwd_in, bwd_in = lax.fori_loop(0, cycle_len - 1, relay, (zero_state, zero_state))
    mixed_rows = []
    grad_rows = []
    gradb_rows = []
    gradc_rows = []
    for seq_id in range(seq_count):
        piece = local_parts[seq_id]
        mixed_h, grad_h, gradb_h, gradc_h = jax.vmap(
            finish, in_axes=(0, 0, 0, 0, 0, 0, 0, 0, None, None, 0, 0)
        )(
            piece[0],
            piece[1],
            piece[2],
            piece[3],
            piece[8],
            piece[9],
            piece[10],
            cot_parts[seq_id],
            b_proj[seq_id],
            c_proj[seq_id],
            fwd_in[seq_id],
            bwd_in[seq_id],
        )
        mixed_rows.append(mixed_h.transpose(1, 0, 2).reshape(block_len, row_width))
        grad_rows.append(grad_h.transpose(1, 0, 2).reshape(block_len, row_width))
        gradb_rows.append(jnp.sum(gradb_h, axis=0))
        gradc_rows.append(jnp.sum(gradc_h, axis=0))
    head_total = lax.psum((jnp.stack(gradb_rows), jnp.stack(gradc_rows)), "heads")
    return (jnp.stack(mixed_rows), jnp.stack(grad_rows), head_total[0], head_total[1])


def solution(mesh):
    placed = (
        P("groups", "seq", "heads"),
        P("groups", "seq", "heads"),
        P("groups", "seq", None),
        P("groups", "seq", None),
        P("groups", "heads", "seq"),
        P("heads"),
        P("groups"),
        P("groups", None),
    )
    return jax.shard_map(
        per_device,
        mesh=mesh,
        in_specs=placed,
        out_specs=(
            P("groups", "seq", "heads"),
            P("groups", "seq", "heads"),
            P("groups", "seq", None),
            P("groups", "seq", None),
        ),
        check_vma=False,
    )
```

profile of v0, /device:TPU:0, one launch (start us, length us, event | category | flops | bytes accessed | tf_op | source)
XLA Modules:
  0.0 1439.0 jit_solution(12802805628567027574)
XLA Ops:
  19.7 4.8 fusion.172
  28.3 4.7 fusion.173
  33.1 4.0 copy.60
  55.7 629.1 %while.75 = (s32[]{:T(128)}, f32[16,1024,64]{1,2,0:T(8,128)}, f32[16,1024,64]{1,2,0:T(8,128)}, f32[16,1024,64]{1,2,0:T(8,128)}, f32[16,1024,64]{1,2,0:T(8,128)},...) while((s32[]{:T(128)}, f32[16,1024,64]{1,2,0:T(8,128)}, ...), condition=%wide.region_6.7_spmd, body=%wide.region_3.6_spmd.sunk | while | flops 736413760 | bytes 37492660 | solution.py:173
  69.7 3.9 multiply_convert_fusion.8
  109.0 3.9 multiply_convert_fusion.8
  148.3 3.9 multiply_convert_fusion.8
  187.6 3.9 multiply_convert_fusion.8
  226.9 3.9 multiply_convert_fusion.8
  266.3 3.9 multiply_convert_fusion.8
  305.6 3.9 multiply_convert_fusion.8
  344.9 3.9 multiply_convert_fusion.8
  423.5 3.9 multiply_convert_fusion.8
  502.2 3.9 multiply_convert_fusion.8
  541.5 3.9 multiply_convert_fusion.8
  580.8 3.9 multiply_convert_fusion.8
  620.2 3.9 multiply_convert_fusion.8
  659.5 3.9 multiply_convert_fusion.8
  685.4 4.0 copy.65
  689.4 4.0 copy.64
  710.7 531.6 %while.76 = (s32[]{:T(128)}, f32[16,1024,64]{1,2,0:T(8,128)}, f32[16,1024,64]{1,2,0:T(8,128)}, f32[16,1024,64]{1,2,0:T(8,128)}, f32[16,1024,64]{1,2,0:T(8,128)},...) while((s32[]{:T(128)}, f32[16,1024,64]{1,2,0:T(8,128)}, ...), condition=%wide.region_13.14_spmd, body=%wide.region_10.13_spmd.sunk | while | flops 736413760 | bytes 37476472 | solution.py:173
  1246.8 94.7 %while.77 = (s32[]{:T(128)}, f32[2,16,64,128]{3,2,1,0:T(8,128)S(1)}, f32[2,16,64,128]{3,2,1,0:T(8,128)S(1)}, f32[2,16]{1,0:T(2,128)S(1)}, f32[2,16,64,128]{3,2,1...) while((s32[]{:T(128)}, ...), condition=%wide.region_15.16_spmd.clone, body=%wide.region_14.15_spmd.clone.sunk | while | flops 2097155 | bytes 27263504 | solution.py:194
  1252.7 19.0 %collective-permute-done = f32[2,16,64,128]{3,2,1,0:T(8,128)S(1)} collective-permute-done((f32[2,16,64,128]{3,2,1,0:T(8,128)}, f32[2,16,64,128]{3,2,1,0:T(8,128)S(1)}, u32[]{:S(2)}, u32[]{:S(2)}) %collective-permute-start) | collective-permute-done | bytes 1048608 | tf_op jit(solution)/shard_map/while/body/eval_jaxpr/ppermute | solution.py:10
  1283.1 17.7 %collective-permute-done = f32[2,16,64,128]{3,2,1,0:T(8,128)S(1)} collective-permute-done((f32[2,16,64,128]{3,2,1,0:T(8,128)}, f32[2,16,64,128]{3,2,1,0:T(8,128)S(1)}, u32[]{:S(2)}, u32[]{:S(2)}) %collective-permute-start) | collective-permute-done | bytes 1048608 | tf_op jit(solution)/shard_map/while/body/eval_jaxpr/ppermute | solution.py:10
  1315.5 16.2 %collective-permute-done = f32[2,16,64,128]{3,2,1,0:T(8,128)S(1)} collective-permute-done((f32[2,16,64,128]{3,2,1,0:T(8,128)}, f32[2,16,64,128]{3,2,1,0:T(8,128)S(1)}, u32[]{:S(2)}, u32[]{:S(2)}) %collective-permute-start) | collective-permute-done | bytes 1048608 | tf_op jit(solution)/shard_map/while/body/eval_jaxpr/ppermute | solution.py:10
  1334.1 4.8 collective-permute-done.1
  1343.6 4.5 fusion.142
  1388.9 4.0 copy.75
  1395.6 5.7 fusion.116
  1401.2 4.1 copy.73
  1405.3 4.2 pad_maximum_fusion.1
  1411.9 16.1 %all-reduce.3.cloned.1.call-done = (f32[2,1024,64]{1,2,0:T(8,128)}, f32[2,1024,64]{1,2,0:T(8,128)}) async-done(((f32[2,1024,64]{1,2,0:T(8,128)}, f32[2,1024,64]{1,2,0:T(8,128)}), (f32[2,1024,64]{1,2,0:T(8,128)}, f32[2,1024,64]{1,2,0:T(8,128)})) %all-reduce.3.cloned.1.call-update) | async-done | bytes 1048592 | tf_op jit(solution)/shard_map/psum | solution.py:221
  (1286 shorter events, 1217.2 us)
Async XLA Ops:
  7.2 9.1 copy-start.27
  7.2 9.1 copy-start.25
  7.2 1420.8 %all-reduce.3.cloned.1.call-start = ((), (), s32[]{:S(2)}) async-start(), calls=%async_computation | async-start | bytes 2097152 | tf_op jit(solution)/shard_map/psum | solution.py:221
  73.7 20.0 %copy-start.44 = (f32[1,1024]{1,0:T(1,128)S(1)}, f32[1,1024]{1,0:T(1,128)}, u32[]{:S(2)}) copy-start(f32[1,1024]{1,0:T(1,128)} %get-tuple-element.1255) | copy-start | bytes 12292 | tf_op jit(solution)/shard_map/while
  113.0 20.0 %copy-start.44 = (f32[1,1024]{1,0:T(1,128)S(1)}, f32[1,1024]{1,0:T(1,128)}, u32[]{:S(2)}) copy-start(f32[1,1024]{1,0:T(1,128)} %get-tuple-element.1255) | copy-start | bytes 12292 | tf_op jit(solution)/shard_map/while
  152.3 20.0 %copy-start.44 = (f32[1,1024]{1,0:T(1,128)S(1)}, f32[1,1024]{1,0:T(1,128)}, u32[]{:S(2)}) copy-start(f32[1,1024]{1,0:T(1,128)} %get-tuple-element.1255) | copy-start | bytes 12292 | tf_op jit(solution)/shard_map/while
  191.6 20.0 %copy-start.44 = (f32[1,1024]{1,0:T(1,128)S(1)}, f32[1,1024]{1,0:T(1,128)}, u32[]{:S(2)}) copy-start(f32[1,1024]{1,0:T(1,128)} %get-tuple-element.1255) | copy-start | bytes 12292 | tf_op jit(solution)/shard_map/while
  230.9 20.0 %copy-start.44 = (f32[1,1024]{1,0:T(1,128)S(1)}, f32[1,1024]{1,0:T(1,128)}, u32[]{:S(2)}) copy-start(f32[1,1024]{1,0:T(1,128)} %get-tuple-element.1255) | copy-start | bytes 12292 | tf_op jit(solution)/shard_map/while
  270.2 20.0 %copy-start.44 = (f32[1,1024]{1,0:T(1,128)S(1)}, f32[1,1024]{1,0:T(1,128)}, u32[]{:S(2)}) copy-start(f32[1,1024]{1,0:T(1,128)} %get-tuple-element.1255) | copy-start | bytes 12292 | tf_op jit(solution)/shard_map/while
  309.5 20.0 %copy-start.44 = (f32[1,1024]{1,0:T(1,128)S(1)}, f32[1,1024]{1,0:T(1,128)}, u32[]{:S(2)}) copy-start(f32[1,1024]{1,0:T(1,128)} %get-tuple-element.1255) | copy-start | bytes 12292 | tf_op jit(solution)/shard_map/while
  348.8 20.0 %copy-start.44 = (f32[1,1024]{1,0:T(1,128)S(1)}, f32[1,1024]{1,0:T(1,128)}, u32[]{:S(2)}) copy-start(f32[1,1024]{1,0:T(1,128)} %get-tuple-element.1255) | copy-start | bytes 12292 | tf_op jit(solution)/shard_map/while
  388.1 20.0 %copy-start.44 = (f32[1,1024]{1,0:T(1,128)S(1)}, f32[1,1024]{1,0:T(1,128)}, u32[]{:S(2)}) copy-start(f32[1,1024]{1,0:T(1,128)} %get-tuple-element.1255) | copy-start | bytes 12292 | tf_op jit(solution)/shard_map/while
  427.5 20.0 %copy-start.44 = (f32[1,1024]{1,0:T(1,128)S(1)}, f32[1,1024]{1,0:T(1,128)}, u32[]{:S(2)}) copy-start(f32[1,1024]{1,0:T(1,128)} %get-tuple-element.1255) | copy-start | bytes 12292 | tf_op jit(solution)/shard_map/while
  466.8 20.0 %copy-start.44 = (f32[1,1024]{1,0:T(1,128)S(1)}, f32[1,1024]{1,0:T(1,128)}, u32[]{:S(2)}) copy-start(f32[1,1024]{1,0:T(1,128)} %get-tuple-element.1255) | copy-start | bytes 12292 | tf_op jit(solution)/shard_map/while
  506.2 20.0 %copy-start.44 = (f32[1,1024]{1,0:T(1,128)S(1)}, f32[1,1024]{1,0:T(1,128)}, u32[]{:S(2)}) copy-start(f32[1,1024]{1,0:T(1,128)} %get-tuple-element.1255) | copy-start | bytes 12292 | tf_op jit(solution)/shard_map/while
  545.5 20.0 %copy-start.44 = (f32[1,1024]{1,0:T(1,128)S(1)}, f32[1,1024]{1,0:T(1,128)}, u32[]{:S(2)}) copy-start(f32[1,1024]{1,0:T(1,128)} %get-tuple-element.1255) | copy-start | bytes 12292 | tf_op jit(solution)/shard_map/while
  584.8 20.0 %copy-start.44 = (f32[1,1024]{1,0:T(1,128)S(1)}, f32[1,1024]{1,0:T(1,128)}, u32[]{:S(2)}) copy-start(f32[1,1024]{1,0:T(1,128)} %get-tuple-element.1255) | copy-start | bytes 12292 | tf_op jit(solution)/shard_map/while
  624.1 20.0 %copy-start.44 = (f32[1,1024]{1,0:T(1,128)S(1)}, f32[1,1024]{1,0:T(1,128)}, u32[]{:S(2)}) copy-start(f32[1,1024]{1,0:T(1,128)} %get-tuple-element.1255) | copy-start | bytes 12292 | tf_op jit(solution)/shard_map/while
  663.4 20.0 %copy-start.44 = (f32[1,1024]{1,0:T(1,128)S(1)}, f32[1,1024]{1,0:T(1,128)}, u32[]{:S(2)}) copy-start(f32[1,1024]{1,0:T(1,128)} %get-tuple-element.1255) | copy-start | bytes 12292 | tf_op jit(solution)/shard_map/while
  710.7 533.7 %copy-start.51 = (f32[16]{0:T(128)S(1)}, f32[16]{0:T(128)}, u32[]{:S(2)}) copy-start(f32[16]{0:T(128)} %get-tuple-element.498) | copy-start | bytes 196
  1249.2 22.5 %collective-permute-start = (f32[2,16,64,128]{3,2,1,0:T(8,128)}, f32[2,16,64,128]{3,2,1,0:T(8,128)S(1)}, u32[]{:S(2)}, u32[]{:S(2)}) collective-permute-start(f32[2,16,64,128]{3,2,1,0:T(8,128)} %fusion.321), channel_id=1, source_target_pairs={{0,1},{1,2},{2,3},{3,0},{4,5},{5,6},{6,7},{7,4},{8,9},{9,10},{10,1... | collective-permute-start | bytes 3145736 | tf_op jit(solution)/shard_map/while/body/eval_jaxpr/ppermute | solution.py:10
  1250.8 24.6 %collective-permute-start.1 = (f32[2,16,64,128]{3,2,1,0:T(8,128)}, f32[2,16,64,128]{3,2,1,0:T(8,128)S(1)}, u32[]{:S(2)}, u32[]{:S(2)}) collective-permute-start(f32[2,16,64,128]{3,2,1,0:T(8,128)} %fusion.322), channel_id=1, source_target_pairs={{0,3},{1,0},{2,1},{3,2},{4,7},{5,4},{6,5},{7,6},{8,11},{9,8},{10,9... | collective-permute-start | bytes 3145736 | tf_op jit(solution)/shard_map/while/body/eval_jaxpr/ppermute | solution.py:10
  1280.2 20.7 %collective-permute-start = (f32[2,16,64,128]{3,2,1,0:T(8,128)}, f32[2,16,64,128]{3,2,1,0:T(8,128)S(1)}, u32[]{:S(2)}, u32[]{:S(2)}) collective-permute-start(f32[2,16,64,128]{3,2,1,0:T(8,128)} %fusion.321), channel_id=1, source_target_pairs={{0,1},{1,2},{2,3},{3,0},{4,5},{5,6},{6,7},{7,4},{8,9},{9,10},{10,1... | collective-permute-start | bytes 3145736 | tf_op jit(solution)/shard_map/while/body/eval_jaxpr/ppermute | solution.py:10
  1282.7 24.2 %collective-permute-start.1 = (f32[2,16,64,128]{3,2,1,0:T(8,128)}, f32[2,16,64,128]{3,2,1,0:T(8,128)S(1)}, u32[]{:S(2)}, u32[]{:S(2)}) collective-permute-start(f32[2,16,64,128]{3,2,1,0:T(8,128)} %fusion.322), channel_id=1, source_target_pairs={{0,3},{1,0},{2,1},{3,2},{4,7},{5,4},{6,5},{7,6},{8,11},{9,8},{10,9... | collective-permute-start | bytes 3145736 | tf_op jit(solution)/shard_map/while/body/eval_jaxpr/ppermute | solution.py:10
  1311.7 20.0 %collective-permute-start = (f32[2,16,64,128]{3,2,1,0:T(8,128)}, f32[2,16,64,128]{3,2,1,0:T(8,128)S(1)}, u32[]{:S(2)}, u32[]{:S(2)}) collective-permute-start(f32[2,16,64,128]{3,2,1,0:T(8,128)} %fusion.321), channel_id=1, source_target_pairs={{0,1},{1,2},{2,3},{3,0},{4,5},{5,6},{6,7},{7,4},{8,9},{9,10},{10,1... | collective-permute-start | bytes 3145736 | tf_op jit(solution)/shard_map/while/body/eval_jaxpr/ppermute | solution.py:10
  1315.5 23.4 %collective-permute-start.1 = (f32[2,16,64,128]{3,2,1,0:T(8,128)}, f32[2,16,64,128]{3,2,1,0:T(8,128)S(1)}, u32[]{:S(2)}, u32[]{:S(2)}) collective-permute-start(f32[2,16,64,128]{3,2,1,0:T(8,128)} %fusion.322), channel_id=1, source_target_pairs={{0,3},{1,0},{2,1},{3,2},{4,7},{5,4},{6,5},{7,6},{8,11},{9,8},{10,9... | collective-permute-start | bytes 3145736 | tf_op jit(solution)/shard_map/while/body/eval_jaxpr/ppermute | solution.py:10
  1350.7 8.9 copy-start.23
  1350.7 22.2 %copy-start.17 = (bf16[16,64,128]{1,2,0:T(8,128)(2,1)}, bf16[16,64,128]{1,2,0:T(8,128)(2,1)S(1)}, u32[]{:S(2)}) copy-start(bf16[16,64,128]{1,2,0:T(8,128)(2,1)S(1)} %get-tuple-element.855) | copy-start | bytes 786436
  1354.5 10.3 copy-start.38
  1354.5 10.3 copy-start.42
  1354.5 13.6 copy-start.36
  1354.6 13.6 copy-start.40
  (93 other events, 327.9 us)
Sparse Core Ops, SparseCore 0:
  1372.3 55.6 all-reduce.2
where the time goes:
time: 1460 us; the launch traced here: 1440 us
  matrix products  573 us (39%)
  other arithmetic  479 us (33%)
  local copies, waits for them, and re-layouts  252 us (17%)
  waiting for transfers between devices  78.8 us (5%)
  loops' own time  27.6 us (2%)
  between operations  21.6 us (1%)
    convert_element_type x32, other arithmetic, block_local(): mixed_gram = (mixing * gram).astype(jnp.bfloat16)  126 us
    dot_general x32, matrix products, block_local(): jnp.dot(mixed_gram, scaled, preferred_element_type=jnp.float32)  98.2 us
    dot_general x32, matrix products, block_local(): inner_prod = jnp.dot(cot_head, scaled.T, preferred_element_type=jnp.float32)  91.5 us
    dot_general x32, matrix products, block_local(): jnp.dot(mixed_gram.T, cot_head, preferred_element_type=jnp.float32)  89.5 us
    dynamic_update_slice x96, other arithmetic, per_device(): lax.map(per_head, (inputs_heads, cot_heads, log_decay[seq_id], skip_gain))  83.4 us
    dynamic_update_slice x96, local copies, waits for them, and re-layouts, per_device(): lax.map(per_head, (inputs_heads, cot_heads, log_decay[seq_id], skip_gain))  67.7 us
    ppermute x6, waiting for transfers between devices, passed_along(): return lax.ppermute(value, axis, pairs)  62.7 us
    another operation x88, local copies, waits for them, and re-layouts  56.2 us
  transfers between devices with their start and end apart: 7, of which 7 were waited for; matrix products, arithmetic and copies ran while one was open for 3% of the time, Pallas kernels for 0%

commit v1 on v0

v1 whole, which is shorter than its diff:
```python
import jax
import jax.numpy as jnp
from jax import lax
from jax.experimental import pallas as pl
from jax.experimental.pallas import tpu as pltpu
from jax.sharding import PartitionSpec as P

Q = 128
LOG2E = 1.4426950408889634
QUANTITIES = 11
A2, E2, SCALE, WH, WM, WG, WL, ALPHA, DELTA, BETA, GAMMA = range(QUANTITIES)
DOC = 2 * QUANTITIES
ROWS = 24
F32 = jnp.float32
BF16 = jnp.bfloat16


def dot(x, y):
    return jnp.dot(x, y, preferred_element_type=F32)


def dot_nt(x, y):
    return lax.dot_general(x, y, (((1,), (1,)), ((), ())), preferred_element_type=F32)


def dot_tn(x, y):
    return lax.dot_general(x, y, (((0,), (0,)), ((), ())), preferred_element_type=F32)


def lane_first(head_dim):
    return lax.broadcasted_iota(jnp.int32, (Q, 2 * head_dim), 1) < head_dim


def spread(cols, quantity, first):
    at = 2 * quantity
    return jnp.where(first, cols[:, at : at + 1], cols[:, at + 1 : at + 2])


def split_heads(pair, first):
    zero = jnp.zeros_like(pair)
    return jnp.concatenate([jnp.where(first, pair, zero), jnp.where(first, zero, pair)], axis=0)


def positions():
    row = lax.broadcasted_iota(jnp.int32, (Q, Q), 0)
    col = lax.broadcasted_iota(jnp.int32, (Q, Q), 1)
    return row, col


def doc_mask(rows, cols, row, col):
    same = cols[:, DOC : DOC + 1] == rows[DOC : DOC + 1, :]
    return jnp.where(same, jnp.where(row == col, 2.0, 1.0), 0.0)


def states_kernel(x_ref, cot_ref, b_ref, c_ref, rows_ref, fac_ref, fwd_ref, bwd_ref, loc_ref):
    chunks = rows_ref.shape[2]
    pair = x_ref.shape[2]
    first = lane_first(pair // 2)
    bx = []
    cc = []
    for k in range(chunks):
        at = pl.ds(k * Q, Q)
        cols = rows_ref[0, 0, k].T
        scaled = (spread(cols, SCALE, first) * x_ref[0, at, :].astype(F32)).astype(BF16).astype(F32)
        cot = cot_ref[0, at, :].astype(F32)
        weighted = jnp.concatenate(
            [
                (spread(cols, WH, first) * scaled).astype(BF16),
                (spread(cols, WG, first) * scaled).astype(BF16),
            ],
            axis=1,
        )
        bx.append(dot_tn(b_ref[0, at, :], weighted))
        weighted = jnp.concatenate(
            [
                (spread(cols, WM, first) * cot).astype(BF16),
                (spread(cols, WL, first) * cot).astype(BF16),
            ],
            axis=1,
        )
        cc.append(dot_tn(c_ref[0, at, :], weighted))
    h = jnp.zeros((bx[0].shape[0], pair), F32)
    m = h
    for k in range(chunks):
        loc_ref[0, 0, k, :, 0:pair] = h.astype(BF16)
        loc_ref[0, 0, k, :, 2 * pair : 3 * pair] = m.astype(BF16)
        f = fac_ref[0, 0, 0, k : k + 1, :]
        h = f * h + bx[k][:, :pair]
        m = f * m + cc[k][:, :pair]
    fwd_ref[0, 0, :, 0:pair] = h
    fwd_ref[0, 0, :, pair : 2 * pair] = m
    g = jnp.zeros_like(h)
    l = g
    for k in reversed(range(chunks)):
        loc_ref[0, 0, k, :, pair : 2 * pair] = g.astype(BF16)
        loc_ref[0, 0, k, :, 3 * pair : 4 * pair] = l.astype(BF16)
        f = fac_ref[0, 0, 1, k : k + 1, :]
        g = f * g + bx[k][:, pair:]
        l = f * l + cc[k][:, pair:]
    bwd_ref[0, 0, :, 0:pair] = g
    bwd_ref[0, 0, :, pair : 2 * pair] = l


def local_grads_kernel(x_ref, cot_ref, b_ref, c_ref, rows_ref, out_ref, total):
    chunks = rows_ref.shape[2]
    first = lane_first(x_ref.shape[2] // 2)
    row, col = positions()
    lower = row >= col
    step = pl.program_id(1)

    @pl.when(step == 0)
    def _():
        total[...] = jnp.zeros_like(total)

    for k in range(chunks):
        at = pl.ds(k * Q, Q)
        rows = rows_ref[0, 0, k]
        cols = rows.T
        scaled = (spread(cols, SCALE, first) * x_ref[0, at, :].astype(F32)).astype(BF16)
        inner = dot_nt(cot_ref[0, at, :], split_heads(scaled, first))
        added = total[k]
        for h in range(2):
            a = 2 * A2 + h
            e = 2 * E2 + h
            decay = jnp.exp2(
                jnp.where(
                    lower,
                    cols[:, a : a + 1] - rows[a : a + 1, :],
                    rows[e : e + 1, :] - cols[:, e : e + 1],
                )
            )
            added = added + decay * inner[:, h * Q : (h + 1) * Q]
        total[k] = added

    @pl.when(step == pl.num_programs(1) - 1)
    def _():
        for k in range(chunks):
            at = pl.ds(k * Q, Q)
            rows = rows_ref[0, 0, k]
            mixed = (total[k] * doc_mask(rows, rows.T, row, col)).astype(BF16)
            grad_b = dot_tn(mixed, c_ref[0, at, :])
            grad_c = dot(mixed, b_ref[0, at, :])
            out_ref[0, at, :] = jnp.concatenate([grad_b, grad_c], axis=1)


def chunk_states(loc_ref, fac_ref, fwd_ref, bwd_ref):
    chunks = loc_ref.shape[2]
    pair = fac_ref.shape[4]
    ahead = []
    factor = jnp.ones((1, pair), F32)
    for k in range(chunks):
        ahead.append(factor)
        factor = factor * fac_ref[0, 0, 0, k : k + 1, :]
    behind = [None] * chunks
    factor = jnp.ones((1, pair), F32)
    for k in reversed(range(chunks)):
        behind[k] = factor
        factor = factor * fac_ref[0, 0, 1, k : k + 1, :]
    states = []
    for k in range(chunks):
        parts = []
        for i, (ref, factors) in enumerate(((fwd_ref, ahead), (bwd_ref, behind)) * 2):
            kept = loc_ref[0, 0, k, :, i * pair : (i + 1) * pair].astype(F32)
            half = (i // 2) * pair
            parts.append((kept + factors[k] * ref[0, 0, :, half : half + pair]).astype(BF16))
        states.append(
            (jnp.concatenate(parts[:2], axis=1), jnp.concatenate(parts[2:], axis=1))
        )
    return states


def far_grads_kernel(x_ref, cot_ref, rows_ref, fac_ref, loc_ref, fwd_ref, bwd_ref, near_ref, out_ref):
    chunks = rows_ref.shape[2]
    first = lane_first(x_ref.shape[2] // 2)
    states = chunk_states(loc_ref, fac_ref, fwd_ref, bwd_ref)

    @pl.when(pl.program_id(1) == 0)
    def _():
        out_ref[...] = near_ref[...]

    for k in range(chunks):
        at = pl.ds(k * Q, Q)
        cols = rows_ref[0, 0, k].T
        scaled = (spread(cols, SCALE, first) * x_ref[0, at, :].astype(F32)).astype(BF16).astype(F32)
        cot = cot_ref[0, at, :].astype(F32)
        state_hg, state_ml = states[k]
        weighted = jnp.concatenate(
            [
                (spread(cols, ALPHA, first) * cot).astype(BF16),
                (spread(cols, BETA, first) * cot).astype(BF16),
            ],
            axis=1,
        )
        grad_c = dot_nt(weighted, state_hg)
        weighted = jnp.concatenate(
            [
                (spread(cols, DELTA, first) * scaled).astype(BF16),
                (spread(cols, GAMMA, first) * scaled).astype(BF16),
            ],
            axis=1,
        )
        grad_b = dot_nt(weighted, state_ml)
        out_ref[0, at, :] += jnp.concatenate([grad_b, grad_c], axis=1)


def rows_out_kernel(
    x_ref, cot_ref, b_ref, c_ref, rows_ref, fac_ref, loc_ref, fwd_ref, bwd_ref, skip_ref,
    mixed_ref, grad_ref, gram, gram_t,
):
    chunks = rows_ref.shape[2]
    pair = x_ref.shape[2]
    first = lane_first(pair // 2)
    row, col = positions()
    states = chunk_states(loc_ref, fac_ref, fwd_ref, bwd_ref)
    skip = skip_ref[0]

    @pl.when(pl.program_id(1) == 0)
    def _():
        for k in range(chunks):
            at = pl.ds(k * Q, Q)
            rows = rows_ref[0, 0, k]
            mask = doc_mask(rows, rows.T, row, col)
            gram[k] = dot_nt(c_ref[0, at, :], b_ref[0, at, :]) * mask
            gram_t[k] = dot_nt(b_ref[0, at, :], c_ref[0, at, :]) * mask

    for k in range(chunks):
        at = pl.ds(k * Q, Q)
        rows = rows_ref[0, 0, k]
        cols = rows.T
        x = x_ref[0, at, :].astype(F32)
        scale = spread(cols, SCALE, first)
        scaled = (scale * x).astype(BF16)
        cot = cot_ref[0, at, :]
        near = []
        near_t = []
        for h in range(2):
            a = 2 * A2 + h
            e = 2 * E2 + h
            a_diff = cols[:, a : a + 1] - rows[a : a + 1, :]
            e_diff = rows[e : e + 1, :] - cols[:, e : e + 1]
            decay = jnp.exp2(jnp.where(row >= col, a_diff, e_diff))
            decay_t = jnp.exp2(-jnp.where(row <= col, a_diff, e_diff))
            near.append((decay * gram[k]).astype(BF16))
            near_t.append((decay_t * gram_t[k]).astype(BF16))
        mixed = dot(jnp.concatenate(near, axis=1), split_heads(scaled, first))
        grad = dot(jnp.concatenate(near_t, axis=1), split_heads(cot, first))
        state_hg, state_ml = states[k]
        far = dot(c_ref[0, at, :], state_hg)
        mixed = mixed + spread(cols, ALPHA, first) * far[:, :pair]
        mixed = mixed + spread(cols, BETA, first) * far[:, pair:]
        mixed_ref[0, at, :] = (mixed + skip * x).astype(BF16)
        far = dot(b_ref[0, at, :], state_ml)
        grad = grad + spread(cols, DELTA, first) * far[:, :pair]
        grad = grad + spread(cols, GAMMA, first) * far[:, pair:]
        grad_ref[0, at, :] = (scale * grad + skip * cot.astype(F32)).astype(BF16)


def exchange(fwd, bwd, factors, core, chip, chips):
    axis = "seq"
    count = 2 * chips
    half = fwd.shape[2] // 2
    swap = [(i, i ^ 1) for i in range(count)]
    own = jnp.stack([fwd, bwd])
    is_even = core == 0
    low, high = own[:, :, :, :half], own[:, :, :, half:]
    mine = jnp.where(is_even, low, high)
    given = jnp.where(is_even, high, low)
    other = lax.ppermute(given, axis, swap)
    even = jnp.where(is_even, mine, other)
    odd = jnp.where(is_even, other, mine)
    factors = factors.reshape((chips, 2) + factors.shape[1:])

    def at(place, direction):
        return lax.dynamic_index_in_dim(factors, jnp.mod(place, chips), 0, keepdims=False)[:, direction]

    here_f = at(chip, 0)
    here_b = at(chip, 1)
    chip_f = odd[0] + here_f[1] * even[0]
    chip_b = even[1] + here_b[0] * odd[1]
    now_f, now_b = chip_f, chip_b
    sum_f = sum_b = None
    weight_f = weight_b = None
    for step in range(1, chips + 1):
        if step < chips:
            now_f = lax.ppermute(now_f, axis, [(i, (i + 2) % count) for i in range(count)])
            now_b = lax.ppermute(now_b, axis, [(i, (i - 2) % count) for i in range(count)])
        else:
            now_f, now_b = chip_f, chip_b
        if step == 1:
            sum_f, sum_b = now_f, now_b
        else:
            sum_f = sum_f + weight_f * now_f
            sum_b = sum_b + weight_b * now_b
        next_f = at(chip - step, 0)
        next_b = at(chip + step, 1)
        next_f = next_f[0] * next_f[1]
        next_b = next_b[0] * next_b[1]
        weight_f = next_f if weight_f is None else weight_f * next_f
        weight_b = next_b if weight_b is None else weight_b * next_b
    into_even = jnp.stack([sum_f, odd[1] + here_b[1] * sum_b])
    into_odd = jnp.stack([even[0] + here_f[0] * sum_f, sum_b])
    kept = jnp.where(is_even, into_even, into_odd)
    got = lax.ppermute(jnp.where(is_even, into_odd, into_even), axis, swap)
    low = jnp.where(is_even, kept, got)
    high = jnp.where(is_even, got, kept)
    return jnp.concatenate([low, high], axis=3)


def per_device(mixer_in, cotangent, b_proj, c_proj, log_decay, skip_gain, offsets, resets):
    seqs, length, width = mixer_in.shape
    heads = log_decay.shape[1]
    head_dim = width // heads
    state = b_proj.shape[2]
    pair = 2 * head_dim
    pairs = heads // 2
    chunks = length // Q
    devices = lax.axis_size("seq")
    place = lax.axis_index("seq")

    block = jnp.mod(place - offsets, devices)
    start = block * length
    bounds = resets[:, None, :]

    def doc_at(position):
        return jnp.sum((position[:, :, None] >= bounds).astype(jnp.int32), axis=2)

    doc = doc_at(start[:, None] + jnp.arange(length, dtype=jnp.int32)[None, :]).reshape(seqs, chunks, Q)
    chunk_start = start[:, None] + Q * jnp.arange(chunks, dtype=jnp.int32)[None, :]
    prev_doc = doc_at(chunk_start - 1)
    next_doc = doc_at(chunk_start + Q)
    first_doc = doc_at(chunk_start)
    last_doc = doc_at(chunk_start + Q - 1)

    decay = log_decay.reshape(seqs, pairs, 2, chunks, Q).transpose(0, 1, 3, 2, 4)
    triangle = (jnp.arange(Q)[:, None] <= jnp.arange(Q)[None, :]).astype(F32)
    cum = jnp.einsum("spkhu,ut->spkht", decay, triangle, precision=lax.Precision.HIGHEST)
    excl = cum - decay
    total = cum[..., Q - 1 :]

    def keep(which):
        return (doc == which[:, :, None]).astype(F32)[:, None, :, None, :]

    keep_last, keep_first, keep_prev, keep_next = map(keep, (last_doc, first_doc, prev_doc, next_doc))
    from_cum, from_excl = jnp.exp(total - cum), jnp.exp(total - excl)
    to_cum, to_excl = jnp.exp(cum), jnp.exp(excl)
    rows = jnp.concatenate(
        [
            cum * LOG2E,
            excl * LOG2E,
            jnp.sqrt(-jnp.expm1(2.0 * decay)),
            from_cum * keep_last,
            from_excl * keep_last,
            to_excl * keep_first,
            to_cum * keep_first,
            to_cum * keep_prev,
            to_excl * keep_prev,
            from_excl * keep_next,
            from_cum * keep_next,
            jnp.broadcast_to(
                doc.astype(F32)[:, None, :, None, :], (seqs, pairs, chunks, ROWS - DOC, Q)
            ),
        ],
        axis=3,
    )
    whole = jnp.exp(total[..., 0])
    passing = jnp.stack([last_doc == prev_doc, first_doc == next_doc], axis=1).astype(F32)
    by_head = whole[:, :, None] * passing[:, None, :, :, None]
    factors = jnp.repeat(by_head, head_dim, axis=-1)

    alive = jnp.stack([block != 0, block != devices - 1]).astype(F32)
    chain = jnp.prod(by_head, axis=3).transpose(2, 0, 1, 3) * alive[:, :, None, None]
    chain = lax.all_gather(chain, "seq")
    chain = jnp.tile(jnp.repeat(chain, head_dim, axis=-1), 2)[..., None, :]

    wide = pl.BlockSpec((1, length, pair), lambda s, p: (s, 0, p))
    thin = pl.BlockSpec((1, length, state), lambda s, p: (s, 0, 0))
    row_spec = pl.BlockSpec((1, 1, chunks, ROWS, Q), lambda s, p: (s, p, 0, 0, 0))
    fac_spec = pl.BlockSpec((1, 1, 2, chunks, pair), lambda s, p: (s, p, 0, 0, 0))
    state_spec = pl.BlockSpec((1, 1, state, 2 * pair), lambda s, p: (s, p, 0, 0))
    loc_spec = pl.BlockSpec((1, 1, chunks, state, 4 * pair), lambda s, p: (s, p, 0, 0, 0))
    sum_spec = pl.BlockSpec((1, length, 2 * state), lambda s, p: (s, 0, 0))
    skip_spec = pl.BlockSpec((1, 1, pair), lambda s, p: (p, 0, 0))
    grid = (seqs, pairs)
    params = pltpu.CompilerParams(vmem_limit_bytes=40 * 2**20)

    def cost(flops, moved):
        return pl.CostEstimate(flops=int(flops), bytes_accessed=int(moved), transcendentals=0)

    area = seqs * length * width
    state_shape = jax.ShapeDtypeStruct((seqs, pairs, state, 2 * pair), F32)
    fwd, bwd, local = pl.pallas_call(
        states_kernel,
        grid=grid,
        in_specs=[wide, wide, thin, thin, row_spec, fac_spec],
        out_specs=[state_spec, state_spec, loc_spec],
        out_shape=[
            state_shape,
            state_shape,
            jax.ShapeDtypeStruct((seqs, pairs, chunks, state, 4 * pair), BF16),
        ],
        compiler_params=params,
        cost_estimate=cost(8 * area * state, 8 * area),
        name="states",
    )(mixer_in, cotangent, b_proj, c_proj, rows, factors)

    near = pl.pallas_call(
        local_grads_kernel,
        grid=grid,
        in_specs=[wide, wide, thin, thin, row_spec],
        out_specs=sum_spec,
        out_shape=jax.ShapeDtypeStruct((seqs, length, 2 * state), F32),
        scratch_shapes=[pltpu.VMEM((chunks, Q, Q), F32)],
        compiler_params=params,
        cost_estimate=cost(6000 * area, 4 * area),
        name="near_grads",
    )(mixer_in, cotangent, b_proj, c_proj, rows)

    incoming = exchange(fwd, bwd, chain, jnp.mod(place, 2), place // 2, devices // 2)
    incoming = incoming * alive[:, :, None, None, None]

    grads = pl.pallas_call(
        far_grads_kernel,
        grid=grid,
        in_specs=[wide, wide, row_spec, fac_spec, loc_spec, state_spec, state_spec, sum_spec],
        out_specs=sum_spec,
        out_shape=jax.ShapeDtypeStruct((seqs, length, 2 * state), F32),
        compiler_params=params,
        cost_estimate=cost(8 * area * state, 8 * area),
        name="far_grads",
    )(mixer_in, cotangent, rows, factors, local, incoming[0], incoming[1], near)
    grads = lax.psum(grads, "heads")

    skip = jnp.repeat(skip_gain.reshape(pairs, 1, 2), head_dim, axis=-1)
    mixed, grad_in = pl.pallas_call(
        rows_out_kernel,
        grid=grid,
        in_specs=[
            wide, wide, thin, thin, row_spec, fac_spec, loc_spec, state_spec, state_spec, skip_spec,
        ],
        out_specs=[wide, wide],
        out_shape=[jax.ShapeDtypeStruct(mixer_in.shape, BF16)] * 2,
        scratch_shapes=[pltpu.VMEM((chunks, Q, Q), F32)] * 2,
        compiler_params=params,
        cost_estimate=cost(12000 * area, 10 * area),
        name="rows_out",
    )(mixer_in, cotangent, b_proj, c_proj, rows, factors, local, incoming[0], incoming[1], skip)
    return mixed, grad_in, grads[..., :state], grads[..., state:]


def solution(mesh):
    placed = (
        P("groups", "seq", "heads"),
        P("groups", "seq", "heads"),
        P("groups", "seq", None),
        P("groups", "seq", None),
        P("groups", "heads", "seq"),
        P("heads"),
        P("groups"),
        P("groups", None),
    )
    return jax.shard_map(
        per_device,
        mesh=mesh,
        in_specs=placed,
        out_specs=(
            P("groups", "seq", "heads"),
            P("groups", "seq", "heads"),
            P("groups", "seq", None),
            P("groups", "seq", None),
        ),
        check_vma=False,
    )
```

time: 1460 us -> 254 us (0.17); the launches traced: 1440 us -> 253 us
  matrix products: 573 us -> 0.21 us
  other arithmetic: 479 us -> 13.2 us
  local copies, waits for them, and re-layouts: 252 us -> 29 us
  Pallas kernels: 0 us -> 165 us
  waiting for transfers between devices: 78.8 us -> 22.2 us
  loops' own time: 27.6 us -> 0 us
    dot_general x306 -> x1, matrix products: 573 us -> 0.21 us  [per_device(): jnp.einsum('spkhu,ut->spkht', decay, triangle, precision=lax.Precision.HI...]
    pallas_call x0 -> x4, Pallas kernels: none -> 165 us  [the longest x1 55.9 us: per_device(): pl.pallas_call(far_grads_kernel, grid=grid, in_specs=[wide, wide, row_spe...]
    mul x166 -> x8, other arithmetic: 140 us -> 1.91 us  [the longest x1 1.26 us: per_device(): to_cum * keep_prev]
    convert_element_type x32 -> x4, other arithmetic: 126 us -> 0.1 us  [the longest x1 0.08 us: keep(): return (doc == which[:, :, None]).astype(F32)[:, None, :, None, :]]
    dynamic_update_slice x96 -> x0, other arithmetic: 83.4 us -> none  [per_device(): lax.map(per_head, (inputs_heads, cot_heads, log_decay[seq_id], skip_gain))]
    another operation x92 -> x2, local copies, waits for them, and re-layouts: 70.8 us -> 0.14 us  [per_device(): chain = jnp.tile(jnp.repeat(chain, head_dim, axis=-1), 2)[..., None, :]]
    slice x75 -> x3, local copies, waits for them, and re-layouts: 71.3 us -> 2.49 us  [the longest x1 2.03 us: per_device(): return (mixed, grad_in, grads[..., :state], grads[..., state:])]
    dynamic_update_slice x96 -> x0, local copies, waits for them, and re-layouts: 67.7 us -> none  [per_device(): lax.map(per_head, (inputs_heads, cot_heads, log_decay[seq_id], skip_gain))]
  transfers between devices with their start and end apart: 7 -> 5, of which waited for: 7 -> 3; matrix products, arithmetic and copies ran while one was open for 3% -> 1% of each run, Pallas kernels for 0% -> 28%
where the time goes in v1:
time: 254 us; the launch traced here: 253 us
  Pallas kernels  165 us (65%)
  local copies, waits for them, and re-layouts  29 us (11%)
  waiting for transfers between devices  22.2 us (9%)
  between operations  14.4 us (6%)
  other arithmetic  13.2 us (5%)
  blocking collectives  6.29 us (2%)
  starting transfers between devices  2.65 us (1%)
    pallas_call x1, Pallas kernels, per_device(): pl.pallas_call(far_grads_kernel, grid=grid, in_specs=[wide, wide, row_spe...  55.9 us
    pallas_call x1, Pallas kernels, per_device(): pl.pallas_call(rows_out_kernel, grid=grid, in_specs=[wide, wide, thin, th...  46.1 us
    pallas_call x1, Pallas kernels, per_device(): pl.pallas_call(states_kernel, grid=grid, in_specs=[wide, wide, thin, thin...  38.1 us
    pallas_call x1, Pallas kernels, per_device(): pl.pallas_call(local_grads_kernel, grid=grid, in_specs=[wide, wide, thin,...  25.1 us
    unnamed x45, local copies, waits for them, and re-layouts  20.7 us
    ppermute x1, waiting for transfers between devices, exchange(): lax.ppermute(now_b, axis, [(i, (i - 2) % count) for i in range(count)])  12.7 us
    ppermute x1, waiting for transfers between devices, exchange(): lax.ppermute(now_f, axis, [(i, (i + 2) % count) for i in range(count)])  8.89 us
    all_gather x1, blocking collectives, per_device(): chain = lax.all_gather(chain, 'seq')  6.29 us
  transfers between devices with their start and end apart: 5, of which 3 were waited for; matrix products, arithmetic and copies ran while one was open for 1% of the time, Pallas kernels for 28%

profile of v1, /device:TPU:0, one launch (start us, length us, event | category | flops | bytes accessed | tf_op | source)
XLA Modules:
  0.0 253.1 jit_solution(3026086672059349331)
XLA Ops:
  7.2 1.3 compare_bitcast_fusion.1
  10.9 0.9 copy.95
  12.4 0.9 copy.94
  13.8 1.0 copy.88.c_ref
  14.8 1.3 exponential_multiply_fusion
  17.2 3.0 %concatenate.18.rows_ref = f32[2,8,8,24,128]{4,3,2,1,0:T(8,128)S(1)} concatenate(f32[2,8,8,2,128]{4,3,2,1,0:T(2,128)S(1)} %get-tuple-element.66, f32[2,8,8,2,128]{4,3,2,1,0:T(2,128)S(1)} %get-tuple-element.64, f32[2,8,8,2,128]{4,3,2,1,0:T(2,128)S(1)} %get-tuple-element.67, f32[2,8,8,2,128]{4,3,2,1,0:T(2,128)S(1)} %get-tuple-element.68, ...), dimensions={3} | concatenate | bytes 3145728 | tf_op jit(solution)/shard_map/concatenate | solution.py:346
  20.2 2.2 copy-done
  22.4 2.2 copy-done.3
  24.6 1.0 copy-done.9
  25.6 38.1 %states.1 = (f32[2,8,64,256]{3,2,1,0:T(8,128)S(1)}, f32[2,8,64,256]{3,2,1,0:T(8,128)S(1)}, bf16[2,8,8,64,512]{4,3,2,1,0:T(8,128)(2,1)}) custom-call(bf16[2,1024,1024]{2,1,0:T(8,128)(2,1)S(1)} %copy-done, bf16[2,1024,1024]{2,1,0:T(8,128)(2,1)S(1)} %copy-done.3, bf16[2,1024,64]{2,1,0:T(8,128)(2,1)S(1)} %copy.87.b_ref, bf16[2,1024,64]{2,1,0:T(8,128)(2,1)S(1)} %copy-done.9, ...), custom_call_target="tpu_custom_call" | custom-call | flops 1073741824 | bytes 16777216 | tf_op jit(solution)/shard_map/states/pallas_call | solution.py:391
  63.8 1.0 copy-done.8
  64.7 1.1 broadcast_select_fusion.5
  66.6 6.3 %all-gather = f32[8,2,8,2]{2,3,1,0:T(2,128)S(1)} all-gather(f32[2,2,8,2]{2,3,1,0:T(2,128)S(1)} %copy.85), channel_id=2, replica_groups=mesh['groups'=2,'heads'=4,'seq'=4] {'seq'}, dimensions={0}, use_global_device_ids=true | all-gather | bytes 1280 | tf_op jit(solution)/shard_map/all_gather | solution.py:372
  73.5 2.1 broadcast_select_fusion.3
  75.6 0.9 copy-done.12
  76.5 1.0 fusion.4
  77.5 1.6 collective-permute-start.2
  79.9 12.7 %collective-permute-done.2 = f32[2,8,32,256]{3,2,1,0:T(8,128)} collective-permute-done((f32[2,8,32,256]{3,2,1,0:T(8,128)}, f32[2,8,32,256]{3,2,1,0:T(8,128)}, u32[]{:S(2)}, u32[]{:S(2)}) %collective-permute-start.2) | collective-permute-done | bytes 524320 | tf_op jit(solution)/shard_map/ppermute | solution.py:286
  92.6 1.7 add_bitcast_fusion.1
  94.3 8.9 %collective-permute-done.1 = f32[2,8,32,256]{3,2,1,0:T(8,128)} collective-permute-done((f32[2,8,32,256]{3,2,1,0:T(8,128)S(1)}, f32[2,8,32,256]{3,2,1,0:T(8,128)}, u32[]{:S(2)}, u32[]{:S(2)}) %collective-permute-start.1) | collective-permute-done | bytes 524320 | tf_op jit(solution)/shard_map/ppermute | solution.py:285
  103.2 1.5 fusion.5
  105.7 25.1 %near_grads.1.near_ref = f32[2,1024,128]{2,1,0:T(8,128)S(1)} custom-call(bf16[2,1024,1024]{2,1,0:T(8,128)(2,1)S(1)} %copy-done.1, bf16[2,1024,1024]{2,1,0:T(8,128)(2,1)S(1)} %copy-done.4, bf16[2,1024,64]{2,1,0:T(8,128)(2,1)S(1)} %copy.87.b_ref, bf16[2,1024,64]{2,1,0:T(8,128)(2,1)S(1)} %copy-done.10, f32[2,8,8,24,128]{4,3,2,1,0:T(8,128)S(1)} %concatenate.18.rows_ref), custom_call_target="tpu_custom_call" | custom-call | flops 12582912000 | bytes 8388608 | tf_op jit(solution)/shard_map/near_grads/pallas_call | solution.py:406
  131.8 55.9 %far_grads.1 = f32[2,1024,128]{2,1,0:T(8,128)} custom-call(bf16[2,1024,1024]{2,1,0:T(8,128)(2,1)S(1)} %copy-done.1, bf16[2,1024,1024]{2,1,0:T(8,128)(2,1)S(1)} %copy-done.4, f32[2,8,8,24,128]{4,3,2,1,0:T(8,128)S(1)} %concatenate.18.rows_ref, f32[2,8,2,8,128]{4,3,2,1,0:T(8,128)S(1)} %reshape.328.fac_ref, ...), custom_call_target="tpu_custom_call" | custom-call | flops 1073741824 | bytes 16777216 | tf_op jit(solution)/shard_map/far_grads/pallas_call | solution.py:421
  187.7 1.0 copy-done.6
  188.7 2.2 copy-done.2
  190.9 2.2 copy-done.5
  193.1 1.2 copy-done.7
  194.3 1.0 copy-done.11
  195.3 46.1 %rows_out.1 = (bf16[2,1024,1024]{2,1,0:T(8,128)(2,1)}, bf16[2,1024,1024]{2,1,0:T(8,128)(2,1)}) custom-call(bf16[2,1024,1024]{2,1,0:T(8,128)(2,1)S(1)} %copy-done.2, bf16[2,1024,1024]{2,1,0:T(8,128)(2,1)S(1)} %copy-done.5, bf16[2,1024,64]{2,1,0:T(8,128)(2,1)S(1)} %copy.87.b_ref, bf16[2,1024,64]{2,1,0:T(8,128)(2,1)S(1)} %copy-done.11, ...), custom_call_target="tpu_custom_call" | custom-call | flops 25165824000 | bytes 20971520 | tf_op jit(solution)/shard_map/rows_out/pallas_call | solution.py:434
  242.0 2.0 fusion.30
  244.1 1.1 copy.91
  245.2 1.1 copy.92
  (83 shorter events, 9.3 us)
Async XLA Ops:
  7.2 6.4 %copy-start.14 = (bf16[2,1024,64]{1,2,0:T(8,128)(2,1)S(1)}, bf16[2,1024,64]{1,2,0:T(8,128)(2,1)}, u32[]{:S(2)}) copy-start(bf16[2,1024,64]{1,2,0:T(8,128)(2,1)} %param.10) | copy-start | bytes 786436
  7.2 6.6 %copy-start.15 = (bf16[2,1024,64]{1,2,0:T(8,128)(2,1)S(1)}, bf16[2,1024,64]{1,2,0:T(8,128)(2,1)}, u32[]{:S(2)}) copy-start(bf16[2,1024,64]{1,2,0:T(8,128)(2,1)} %param.11) | copy-start | bytes 786436
  7.2 234.9 %all-reduce.2.cloned.1.call-start = ((), (), s32[]{:S(2)}) async-start(), calls=%async_computation | async-start | bytes 2097152 | tf_op jit(solution)/shard_map/psum | solution.py:431
  8.5 0.6 copy-start.18
  20.2 2.2 copy-start
  22.4 2.2 copy-start.3
  24.6 1.0 copy-start.9
  63.8 1.0 copy-start.8
  63.8 2.5 %copy-start.19 = (s32[2]{0:T(128)S(1)}, s32[2]{0:T(128)}, u32[]{:S(2)}) copy-start(s32[2]{0:T(128)} %copy-done.18) | copy-start | bytes 28
  63.8 2.5 %copy-start.16 = (pred[1,2]{1,0:T(4,128)(4,1)S(1)}, pred[1,2]{1,0:T(4,128)(4,1)}, u32[]{:S(2)}) copy-start(pred[1,2]{1,0:T(4,128)(4,1)} %get-tuple-element.38) | copy-start | bytes 10
  65.8 7.6 %collective-permute-start = (f32[2,2,8,32,256]{4,3,2,1,0:T(8,128)}, f32[2,2,8,32,256]{4,3,2,1,0:T(8,128)}, u32[]{:S(2)}, u32[]{:S(2)}) collective-permute-start(f32[2,2,8,32,256]{4,3,2,1,0:T(8,128)} %broadcast_select_fusion.5), channel_id=1, source_target_pairs={{0,1},{1,0},{2,3},{3,2},{4,5},{5,4},{6,7},{7,6},{8,9},{9,8},{10,11... | collective-permute-start | bytes 3145736 | tf_op jit(solution)/shard_map/ppermute | solution.py:268
  75.5 1.0 copy-start.12
  75.5 2.0 copy-start.13
  75.6 4.1 %copy-start.17 = (f32[16]{0:T(128)S(1)}, f32[16]{0:T(128)}, u32[]{:S(2)}) copy-start(f32[16]{0:T(128)} %param.13) | copy-start | bytes 196
  76.5 28.5 %copy-start.10 = (bf16[2,1024,64]{2,1,0:T(8,128)(2,1)S(1)}, bf16[2,1024,64]{2,1,0:T(8,128)(2,1)}, u32[]{:S(2)}) copy-start(bf16[2,1024,64]{2,1,0:T(8,128)(2,1)} %copy.88.c_ref) | copy-start | bytes 786436
  77.5 15.1 %collective-permute-start.2 = (f32[2,8,32,256]{3,2,1,0:T(8,128)}, f32[2,8,32,256]{3,2,1,0:T(8,128)}, u32[]{:S(2)}, u32[]{:S(2)}) collective-permute-start(f32[2,8,32,256]{3,2,1,0:T(8,128)} %get-tuple-element.49), channel_id=1, source_target_pairs={{0,2},{1,3},{2,0},{3,1},{4,6},{5,7},{6,4},{7,5},{8,10},{9,11},{10,... | collective-permute-start | bytes 1572872 | tf_op jit(solution)/shard_map/ppermute | solution.py:286
  79.1 24.1 %collective-permute-start.1 = (f32[2,8,32,256]{3,2,1,0:T(8,128)S(1)}, f32[2,8,32,256]{3,2,1,0:T(8,128)}, u32[]{:S(2)}, u32[]{:S(2)}) collective-permute-start(f32[2,8,32,256]{3,2,1,0:T(8,128)S(1)} %get-tuple-element.48), channel_id=1, source_target_pairs={{0,2},{1,3},{2,0},{3,1},{4,6},{5,7},{6,4},{7,5},{8,10},{9,11},{10,... | collective-permute-start | bytes 1572872 | tf_op jit(solution)/shard_map/ppermute | solution.py:285
  92.6 12.4 %copy-start.4 = (bf16[2,1024,1024]{2,1,0:T(8,128)(2,1)S(1)}, bf16[2,1024,1024]{2,1,0:T(8,128)(2,1)}, u32[]{:S(2)}) copy-start(bf16[2,1024,1024]{2,1,0:T(8,128)(2,1)} %cot_ref.7) | copy-start | bytes 12582916
  103.2 2.5 copy-start.1
  104.9 25.9 %collective-permute-start.3 = (f32[2,2,8,32,256]{4,3,2,1,0:T(8,128)S(1)}, f32[2,2,8,32,256]{4,3,2,1,0:T(8,128)S(1)}, u32[]{:S(2)}, u32[]{:S(2)}) collective-permute-start(f32[2,2,8,32,256]{4,3,2,1,0:T(8,128)S(1)} %fusion.1), channel_id=1, source_target_pairs={{0,1},{1,0},{2,3},{3,2},{4,5},{5,4},{6,7},{7,6},{8,9},{9,8},{10,11... | collective-permute-start | bytes 3145736 | tf_op jit(solution)/shard_map/ppermute | solution.py:303
  187.7 1.0 copy-start.6
  188.7 2.2 copy-start.2
  190.9 2.2 copy-start.5
  193.1 1.2 copy-start.7
  194.3 1.0 copy-start.11
Sparse Core Ops, SparseCore 0:
  188.8 53.1 all-reduce.1

commit v2 on v1

--- a/solution.py
+++ b/solution.py
@@ -1,3 +1,5 @@
+import numpy as np
+
 import jax
 import jax.numpy as jnp
 from jax import lax
@@ -31,9 +33,25 @@
     return lax.broadcasted_iota(jnp.int32, (Q, 2 * head_dim), 1) < head_dim
 
 
-def spread(cols, quantity, first):
-    at = 2 * quantity
-    return jnp.where(first, cols[:, at : at + 1], cols[:, at + 1 : at + 2])
+def selector(wanted, head_dim):
+    out = np.zeros((ROWS, len(wanted), 2 * head_dim), np.float32)
+    for i, (quantity, head) in enumerate(wanted):
+        if head is None:
+            out[2 * quantity, i, :head_dim] = 1.0
+            out[2 * quantity + 1, i, head_dim:] = 1.0
+        else:
+            out[2 * quantity + head, i, :] = 1.0
+    out = out.reshape(ROWS, -1)
+    return jnp.asarray(np.concatenate([out] * 3, axis=0), BF16)
+
+
+def columns(rows, select_ref):
+    high = rows.astype(BF16).astype(F32)
+    rest = rows - high
+    middle = rest.astype(BF16).astype(F32)
+    parts = jnp.concatenate([high, middle, rest - middle], axis=0).astype(BF16)
+    spread = dot_tn(parts, select_ref[...])
+    return [spread[:, i : i + Q] for i in range(0, spread.shape[1], Q)]
 
 
 def split_heads(pair, first):
@@ -52,29 +70,28 @@
     return jnp.where(same, jnp.where(row == col, 2.0, 1.0), 0.0)
 
 
-def states_kernel(x_ref, cot_ref, b_ref, c_ref, rows_ref, fac_ref, fwd_ref, bwd_ref, loc_ref):
+def states_kernel(x_ref, cot_ref, b_ref, c_ref, rows_ref, fac_ref, select_ref, fwd_ref, bwd_ref, loc_ref):
     chunks = rows_ref.shape[2]
     pair = x_ref.shape[2]
-    first = lane_first(pair // 2)
     bx = []
     cc = []
     for k in range(chunks):
         at = pl.ds(k * Q, Q)
-        cols = rows_ref[0, 0, k].T
-        scaled = (spread(cols, SCALE, first) * x_ref[0, at, :].astype(F32)).astype(BF16).astype(F32)
+        scale, w_h, w_g, w_m, w_l = columns(rows_ref[0, 0, k], select_ref)
+        scaled = (scale * x_ref[0, at, :].astype(F32)).astype(BF16).astype(F32)
         cot = cot_ref[0, at, :].astype(F32)
         weighted = jnp.concatenate(
             [
-                (spread(cols, WH, first) * scaled).astype(BF16),
-                (spread(cols, WG, first) * scaled).astype(BF16),
+                (w_h * scaled).astype(BF16),
+                (w_g * scaled).astype(BF16),
             ],
             axis=1,
         )
         bx.append(dot_tn(b_ref[0, at, :], weighted))
         weighted = jnp.concatenate(
             [
-                (spread(cols, WM, first) * cot).astype(BF16),
-                (spread(cols, WL, first) * cot).astype(BF16),
+                (w_m * cot).astype(BF16),
+                (w_l * cot).astype(BF16),
             ],
             axis=1,
         )
@@ -101,7 +118,7 @@
     bwd_ref[0, 0, :, pair : 2 * pair] = l
 
 
-def local_grads_kernel(x_ref, cot_ref, b_ref, c_ref, rows_ref, out_ref, total):
+def local_grads_kernel(x_ref, cot_ref, b_ref, c_ref, rows_ref, select_ref, out_ref, total):
     chunks = rows_ref.shape[2]
     first = lane_first(x_ref.shape[2] // 2)
     row, col = positions()
@@ -115,8 +132,8 @@
     for k in range(chunks):
         at = pl.ds(k * Q, Q)
         rows = rows_ref[0, 0, k]
-        cols = rows.T
-        scaled = (spread(cols, SCALE, first) * x_ref[0, at, :].astype(F32)).astype(BF16)
+        scale, *sides = columns(rows, select_ref)
+        scaled = (scale * x_ref[0, at, :].astype(F32)).astype(BF16)
         inner = dot_nt(cot_ref[0, at, :], split_heads(scaled, first))
         added = total[k]
         for h in range(2):
@@ -125,8 +142,8 @@
             decay = jnp.exp2(
                 jnp.where(
                     lower,
-                    cols[:, a : a + 1] - rows[a : a + 1, :],
-                    rows[e : e + 1, :] - cols[:, e : e + 1],
+                    sides[h] - rows[a : a + 1, :],
+                    rows[e : e + 1, :] - sides[2 + h],
                 )
             )
             added = added + decay * inner[:, h * Q : (h + 1) * Q]
@@ -169,9 +186,10 @@
     return states
 
 
-def far_grads_kernel(x_ref, cot_ref, rows_ref, fac_ref, loc_ref, fwd_ref, bwd_ref, near_ref, out_ref):
+def far_grads_kernel(
+    x_ref, cot_ref, rows_ref, fac_ref, loc_ref, fwd_ref, bwd_ref, near_ref, select_ref, out_ref
+):
     chunks = rows_ref.shape[2]
-    first = lane_first(x_ref.shape[2] // 2)
     states = chunk_states(loc_ref, fac_ref, fwd_ref, bwd_ref)
 
     @pl.when(pl.program_id(1) == 0)
@@ -180,22 +198,22 @@
 
     for k in range(chunks):
         at = pl.ds(k * Q, Q)
-        cols = rows_ref[0, 0, k].T
-        scaled = (spread(cols, SCALE, first) * x_ref[0, at, :].astype(F32)).astype(BF16).astype(F32)
+        scale, alpha, beta, delta, gamma = columns(rows_ref[0, 0, k], select_ref)
+        scaled = (scale * x_ref[0, at, :].astype(F32)).astype(BF16).astype(F32)
         cot = cot_ref[0, at, :].astype(F32)
         state_hg, state_ml = states[k]
         weighted = jnp.concatenate(
             [
-                (spread(cols, ALPHA, first) * cot).astype(BF16),
-                (spread(cols, BETA, first) * cot).astype(BF16),
+                (alpha * cot).astype(BF16),
+                (beta * cot).astype(BF16),
             ],
             axis=1,
         )
         grad_c = dot_nt(weighted, state_hg)
         weighted = jnp.concatenate(
             [
-                (spread(cols, DELTA, first) * scaled).astype(BF16),
-                (spread(cols, GAMMA, first) * scaled).astype(BF16),
+                (delta * scaled).astype(BF16),
+                (gamma * scaled).astype(BF16),
             ],
             axis=1,
         )
@@ -204,7 +222,7 @@
 
 
 def rows_out_kernel(
-    x_ref, cot_ref, b_ref, c_ref, rows_ref, fac_ref, loc_ref, fwd_ref, bwd_ref, skip_ref,
+    x_ref, cot_ref, b_ref, c_ref, rows_ref, fac_ref, loc_ref, fwd_ref, bwd_ref, skip_ref, select_ref,
     mixed_ref, grad_ref, gram, gram_t,
 ):
     chunks = rows_ref.shape[2]
@@ -226,9 +244,8 @@
     for k in range(chunks):
         at = pl.ds(k * Q, Q)
         rows = rows_ref[0, 0, k]
-        cols = rows.T
+        scale, alpha, beta, delta, gamma, *sides = columns(rows, select_ref)
         x = x_ref[0, at, :].astype(F32)
-        scale = spread(cols, SCALE, first)
         scaled = (scale * x).astype(BF16)
         cot = cot_ref[0, at, :]
         near = []
@@ -236,8 +253,8 @@
         for h in range(2):
             a = 2 * A2 + h
             e = 2 * E2 + h
-            a_diff = cols[:, a : a + 1] - rows[a : a + 1, :]
-            e_diff = rows[e : e + 1, :] - cols[:, e : e + 1]
+            a_diff = sides[h] - rows[a : a + 1, :]
+            e_diff = rows[e : e + 1, :] - sides[2 + h]
             decay = jnp.exp2(jnp.where(row >= col, a_diff, e_diff))
             decay_t = jnp.exp2(-jnp.where(row <= col, a_diff, e_diff))
             near.append((decay * gram[k]).astype(BF16))
@@ -246,16 +263,16 @@
         grad = dot(jnp.concatenate(near_t, axis=1), split_heads(cot, first))
         state_hg, state_ml = states[k]
         far = dot(c_ref[0, at, :], state_hg)
-        mixed = mixed + spread(cols, ALPHA, first) * far[:, :pair]
-        mixed = mixed + spread(cols, BETA, first) * far[:, pair:]
+        mixed = mixed + alpha * far[:, :pair]
+        mixed = mixed + beta * far[:, pair:]
         mixed_ref[0, at, :] = (mixed + skip * x).astype(BF16)
         far = dot(b_ref[0, at, :], state_ml)
-        grad = grad + spread(cols, DELTA, first) * far[:, :pair]
-        grad = grad + spread(cols, GAMMA, first) * far[:, pair:]
+        grad = grad + delta * far[:, :pair]
+        grad = grad + gamma * far[:, pair:]
         grad_ref[0, at, :] = (scale * grad + skip * cot.astype(F32)).astype(BF16)
 
 
-def exchange(fwd, bwd, factors, core, chip, chips):
+def exchange(fwd, bwd, factors, core, chips, meanwhile):
     axis = "seq"
     count = 2 * chips
     half = fwd.shape[2] // 2
@@ -268,15 +285,17 @@
     other = lax.ppermute(given, axis, swap)
     even = jnp.where(is_even, mine, other)
     odd = jnp.where(is_even, other, mine)
-    factors = factors.reshape((chips, 2) + factors.shape[1:])
-
-    def at(place, direction):
-        return lax.dynamic_index_in_dim(factors, jnp.mod(place, chips), 0, keepdims=False)[:, direction]
-
-    here_f = at(chip, 0)
-    here_b = at(chip, 1)
+    def at(hops, direction):
+        return [
+            jnp.where(is_even, factors[(2 * hops - k) % count], factors[(2 * hops + 1 - k) % count])[direction]
+            for k in range(2)
+        ]
+
+    here_f = at(0, 0)
+    here_b = at(0, 1)
     chip_f = odd[0] + here_f[1] * even[0]
     chip_b = even[1] + here_b[0] * odd[1]
+    near, (chip_f, chip_b) = meanwhile((chip_f, chip_b))
     now_f, now_b = chip_f, chip_b
     sum_f = sum_b = None
     weight_f = weight_b = None
@@ -284,6 +303,8 @@
         if step < chips:
             now_f = lax.ppermute(now_f, axis, [(i, (i + 2) % count) for i in range(count)])
             now_b = lax.ppermute(now_b, axis, [(i, (i - 2) % count) for i in range(count)])
+            if step == 1:
+                now_f, now_b, near = lax.optimization_barrier((now_f, now_b, near))
         else:
             now_f, now_b = chip_f, chip_b
         if step == 1:
@@ -291,8 +312,8 @@
         else:
             sum_f = sum_f + weight_f * now_f
             sum_b = sum_b + weight_b * now_b
-        next_f = at(chip - step, 0)
-        next_b = at(chip + step, 1)
+        next_f = at(step, 0)
+        next_b = at(-step, 1)
         next_f = next_f[0] * next_f[1]
         next_b = next_b[0] * next_b[1]
         weight_f = next_f if weight_f is None else weight_f * next_f
@@ -303,7 +324,7 @@
     got = lax.ppermute(jnp.where(is_even, into_odd, into_even), axis, swap)
     low = jnp.where(is_even, kept, got)
     high = jnp.where(is_even, got, kept)
-    return jnp.concatenate([low, high], axis=3)
+    return jnp.concatenate([low, high], axis=3), near
 
 
 def per_device(mixer_in, cotangent, b_proj, c_proj, log_decay, skip_gain, offsets, resets):
@@ -369,8 +390,11 @@
 
     alive = jnp.stack([block != 0, block != devices - 1]).astype(F32)
     chain = jnp.prod(by_head, axis=3).transpose(2, 0, 1, 3) * alive[:, :, None, None]
-    chain = lax.all_gather(chain, "seq")
-    chain = jnp.tile(jnp.repeat(chain, head_dim, axis=-1), 2)[..., None, :]
+    around = [chain] + [
+        lax.ppermute(chain, "seq", [(i, (i + shift) % devices) for i in range(devices)])
+        for shift in range(1, devices)
+    ]
+    chain = jnp.tile(jnp.repeat(jnp.stack(around), head_dim, axis=-1), 2)[..., None, :]
 
     wide = pl.BlockSpec((1, length, pair), lambda s, p: (s, 0, p))
     thin = pl.BlockSpec((1, length, state), lambda s, p: (s, 0, 0))
@@ -381,17 +405,29 @@
     sum_spec = pl.BlockSpec((1, length, 2 * state), lambda s, p: (s, 0, 0))
     skip_spec = pl.BlockSpec((1, 1, pair), lambda s, p: (p, 0, 0))
     grid = (seqs, pairs)
-    params = pltpu.CompilerParams(vmem_limit_bytes=40 * 2**20)
+    params = pltpu.CompilerParams(vmem_limit_bytes=60 * 2**20)
 
     def cost(flops, moved):
         return pl.CostEstimate(flops=int(flops), bytes_accessed=int(moved), transcendentals=0)
+
+    def select(*wanted):
+        matrix = selector(wanted, head_dim)
+        return matrix, pl.BlockSpec(matrix.shape, lambda s, p: (0, 0))
+
+    scale = [(SCALE, None)]
+    far_factors = [(q, None) for q in (ALPHA, BETA, DELTA, GAMMA)]
+    sides = [(A2, 0), (A2, 1), (E2, 0), (E2, 1)]
+    states_sel, states_spec = select(*scale, *[(q, None) for q in (WH, WG, WM, WL)])
+    near_sel, near_spec = select(*scale, *sides)
+    far_sel, far_spec = select(*scale, *far_factors)
+    out_sel, out_spec = select(*scale, *far_factors, *sides)
 
     area = seqs * length * width
     state_shape = jax.ShapeDtypeStruct((seqs, pairs, state, 2 * pair), F32)
     fwd, bwd, local = pl.pallas_call(
         states_kernel,
         grid=grid,
-        in_specs=[wide, wide, thin, thin, row_spec, fac_spec],
+        in_specs=[wide, wide, thin, thin, row_spec, fac_spec, states_spec],
         out_specs=[state_spec, state_spec, loc_spec],
         out_shape=[
             state_shape,
@@ -399,35 +435,41 @@
             jax.ShapeDtypeStruct((seqs, pairs, chunks, state, 4 * pair), BF16),
         ],
         compiler_params=params,
-        cost_estimate=cost(8 * area * state, 8 * area),
+        cost_estimate=cost(5000 * area, 8 * area),
         name="states",
-    )(mixer_in, cotangent, b_proj, c_proj, rows, factors)
-
-    near = pl.pallas_call(
+    )(mixer_in, cotangent, b_proj, c_proj, rows, factors, states_sel)
+
+    near_call = pl.pallas_call(
         local_grads_kernel,
         grid=grid,
-        in_specs=[wide, wide, thin, thin, row_spec],
+        in_specs=[wide, wide, thin, thin, row_spec, near_spec],
         out_specs=sum_spec,
         out_shape=jax.ShapeDtypeStruct((seqs, length, 2 * state), F32),
         scratch_shapes=[pltpu.VMEM((chunks, Q, Q), F32)],
         compiler_params=params,
         cost_estimate=cost(6000 * area, 4 * area),
         name="near_grads",
-    )(mixer_in, cotangent, b_proj, c_proj, rows)
-
-    incoming = exchange(fwd, bwd, chain, jnp.mod(place, 2), place // 2, devices // 2)
+    )
+
+    def near_grads(token):
+        held, token = lax.optimization_barrier((rows, token))
+        return near_call(mixer_in, cotangent, b_proj, c_proj, held, near_sel), token
+
+    incoming, near = exchange(
+        fwd, bwd, chain, jnp.mod(place, 2), devices // 2, near_grads
+    )
     incoming = incoming * alive[:, :, None, None, None]
 
     grads = pl.pallas_call(
         far_grads_kernel,
         grid=grid,
-        in_specs=[wide, wide, row_spec, fac_spec, loc_spec, state_spec, state_spec, sum_spec],
+        in_specs=[wide, wide, row_spec, fac_spec, loc_spec, state_spec, state_spec, sum_spec, far_spec],
         out_specs=sum_spec,
         out_shape=jax.ShapeDtypeStruct((seqs, length, 2 * state), F32),
         compiler_params=params,
-        cost_estimate=cost(8 * area * state, 8 * area),
+        cost_estimate=cost(5000 * area, 8 * area),
         name="far_grads",
-    )(mixer_in, cotangent, rows, factors, local, incoming[0], incoming[1], near)
+    )(mixer_in, cotangent, rows, factors, local, incoming[0], incoming[1], near, far_sel)
     grads = lax.psum(grads, "heads")
 
     skip = jnp.repeat(skip_gain.reshape(pairs, 1, 2), head_dim, axis=-1)
@@ -435,7 +477,7 @@
         rows_out_kernel,
         grid=grid,
         in_specs=[
-            wide, wide, thin, thin, row_spec, fac_spec, loc_spec, state_spec, state_spec, skip_spec,
+            wide, wide, thin, thin, row_spec, fac_spec, loc_spec, state_spec, state_spec, skip_spec, out_spec,
         ],
         out_specs=[wide, wide],
         out_shape=[jax.ShapeDtypeStruct(mixer_in.shape, BF16)] * 2,
@@ -443,7 +485,7 @@
         compiler_params=params,
         cost_estimate=cost(12000 * area, 10 * area),
         name="rows_out",
-    )(mixer_in, cotangent, b_proj, c_proj, rows, factors, local, incoming[0], incoming[1], skip)
+    )(mixer_in, cotangent, b_proj, c_proj, rows, factors, local, incoming[0], incoming[1], skip, out_sel)
     return mixed, grad_in, grads[..., :state], grads[..., state:]
 
 

time: 254 us -> 193 us (0.76)
  Pallas kernels: 165 us -> 127 us
  local copies, waits for them, and re-layouts: 29 us -> 18.4 us
  waiting for transfers between devices: 22.2 us -> 15.1 us
  blocking collectives: 6.29 us -> 0 us
  starting transfers between devices: 2.65 us -> 6.68 us
    pallas_call x1, Pallas kernels: 55.9 us -> 32.4 us  [per_device(): pl.pallas_call(far_grads_kernel, grid=grid, in_specs=[wide, wide, row_spe...]
    unnamed x45 -> x21, local copies, waits for them, and re-layouts: 20.7 us -> 6.36 us
    ppermute x1, waiting for transfers between devices: 12.7 us -> 0.01 us  [exchange(): lax.ppermute(now_b, axis, [(i, (i - 2) % count) for i in range(count)])]
    psum x1, waiting for transfers between devices: 0.62 us -> 11.9 us  [per_device(): grads = lax.psum(grads, 'heads')]
    ppermute x1, waiting for transfers between devices: 8.89 us -> 0.01 us  [exchange(): lax.ppermute(now_f, axis, [(i, (i + 2) % count) for i in range(count)])]
    pallas_call x1, Pallas kernels: 38.1 us -> 31 us  [per_device(): pl.pallas_call(states_kernel, grid=grid, in_specs=[wide, wide, thin, thin...]
    all_gather x1 -> x0, blocking collectives: 6.29 us -> none  [per_device(): chain = lax.all_gather(chain, 'seq')]
    pallas_call x1, Pallas kernels: 46.1 us -> 40.4 us  [per_device(): pl.pallas_call(rows_out_kernel, grid=grid, in_specs=[wide, wide, thin, th...]
  transfers between devices with their start and end apart: 5 -> 8, of which waited for: 3 -> 3; matrix products, arithmetic and copies ran while one was open for 1% -> 7% of each run, Pallas kernels for 28% -> 49%
where the time goes in v2:
time: 193 us; the launch traced here: 192 us
  Pallas kernels  127 us (66%)
  local copies, waits for them, and re-layouts  18.4 us (10%)
  waiting for transfers between devices  15.1 us (8%)
  between operations  14.4 us (7%)
  other arithmetic  10.7 us (6%)
  starting transfers between devices  6.68 us (3%)
    pallas_call x1, Pallas kernels, per_device(): pl.pallas_call(rows_out_kernel, grid=grid, in_specs=[wide, wide, thin, th...  40.4 us
    pallas_call x1, Pallas kernels, per_device(): pl.pallas_call(far_grads_kernel, grid=grid, in_specs=[wide, wide, row_spe...  32.4 us
    pallas_call x1, Pallas kernels, per_device(): pl.pallas_call(states_kernel, grid=grid, in_specs=[wide, wide, thin, thin...  31 us
    pallas_call x1, Pallas kernels, near_grads(): near_call(mixer_in, cotangent, b_proj, c_proj, held, near_sel)  23.2 us
    psum x1, waiting for transfers between devices, per_device(): grads = lax.psum(grads, 'heads')  11.9 us
    unnamed x21, local copies, waits for them, and re-layouts  6.36 us
    ppermute x3, starting transfers between devices, per_device(): lax.ppermute(chain, 'seq', [(i, (i + shift) % devices) for i in range(dev...  4.41 us
  transfers between devices with their start and end apart: 8, of which 3 were waited for; matrix products, arithmetic and copies ran while one was open for 7% of the time, Pallas kernels for 49%

profile of v2, /device:TPU:0, one launch (start us, length us, event | category | flops | bytes accessed | tf_op | source)
XLA Modules:
  0.0 192.4 jit_solution(11735672650568222014)
XLA Ops:
  7.3 0.7 compare_bitcast_fusion.1
  8.2 0.8 fusion.24
  9.0 0.9 copy.147
  11.1 0.5 collective-permute-start.2
  11.6 2.6 %collective-permute-start.5 = (f32[2,2,8,2]{3,0,2,1:T(2,128)S(1)}, f32[2,2,8,2]{3,0,2,1:T(2,128)S(1)}, u32[]{:S(2)}, u32[]{:S(2)}) collective-permute-start(f32[2,2,8,2]{3,0,2,1:T(2,128)S(1)} %bitcast_multiply_fusion), channel_id=1, source_target_pairs={{0,2},{1,3},{2,0},{3,1},{4,6},{5,7},{6,4},{7,5},{8,10},{9,11},{10,... | collective-permute-start | bytes 776 | tf_op jit(solution)/shard_map/ppermute | solution.py:394
  14.1 1.4 collective-permute-start.1
  15.8 0.9 copy.140
  17.0 0.9 reshape.535.fac_ref
  17.9 1.0 copy.135.b_ref
  18.9 1.0 copy.136.c_ref
  19.9 0.6 exponential_multiply_fusion
  20.7 3.6 %concatenate.18.rows_ref = f32[2,8,8,24,128]{4,3,2,1,0:T(8,128)} concatenate(f32[2,8,8,2,128]{4,3,2,1,0:T(2,128)S(1)} %get-tuple-element.76, f32[2,8,8,2,128]{4,3,2,1,0:T(2,128)S(1)} %get-tuple-element.74, f32[2,8,8,2,128]{4,3,2,1,0:T(2,128)S(1)} %get-tuple-element.77, f32[2,8,8,2,128]{4,3,2,1,0:T(2,128)S(1)} %get-tuple-element.78, f32[2,8,8,2,128]{4,3,2,1,0:T(2,128)S(1)} %get-tuple-element.73, ...), dimensions={3} | concatenate | bytes 3145728 | tf_op jit(solution)/shard_map/concatenate | solution.py:367
  24.4 31.0 %states.1 = (f32[2,8,64,256]{3,2,1,0:T(8,128)}, f32[2,8,64,256]{3,2,1,0:T(8,128)}, bf16[2,8,8,64,512]{4,3,2,1,0:T(8,128)(2,1)}) custom-call(bf16[2,1024,1024]{2,1,0:T(8,128)(2,1)} %x_ref.7, bf16[2,1024,1024]{2,1,0:T(8,128)(2,1)} %cot_ref.7, bf16[2,1024,64]{2,1,0:T(8,128)(2,1)} %copy.135.b_ref, bf16[2,1024,64]{2,1,0:T(8,128)(2,1)} %copy.136.c_ref, ...), custom_call_target="tpu_custom_call" | custom-call | flops 10485760000 | bytes 16777216 | tf_op jit(solution)/shard_map/states/pallas_call | solution.py:427
  55.4 1.8 broadcast_select_fusion.5
  58.4 1.5 collective-permute-done
  60.0 2.0 %broadcast_select_fusion.2 = (f32[2,2,8,32,256]{4,3,2,1,0:T(8,128)S(1)}, f32[2,2,8,32,256]{4,3,2,1,0:T(8,128)S(1)}) fusion(f32[2,2,8,32,256]{4,3,2,1,0:T(8,128)} %collective-permute-done, pred[]{:T(512)S(6)} %eq.97, f32[1,2,8,64,256]{4,3,2,1,0:T(8,128)} %bitcast.118, f32[1,2,8,64,256]{4,3,2,1,0:T(8,128)S(1)} %bitcast.116), kind=kLoop, calls=%fused_computation.23 | loop fusion | flops 1835008 | bytes 5242881 | tf_op jit(solution)/shard_map/jit(_where)/select_n | solution.py:286
  62.3 0.4 collective-permute-start.3
  62.7 1.7 collective-permute-start.4
  64.4 23.2 %near_grads.1.near_ref = f32[2,1024,128]{2,1,0:T(8,128)} custom-call(bf16[2,1024,1024]{2,1,0:T(8,128)(2,1)} %x_ref.7, bf16[2,1024,1024]{2,1,0:T(8,128)(2,1)} %cot_ref.7, bf16[2,1024,64]{2,1,0:T(8,128)(2,1)} %copy.135.b_ref, bf16[2,1024,64]{2,1,0:T(8,128)(2,1)} %copy.136.c_ref, f32[2,8,8,24,128]{4,3,2,1,0:T(8,128)} %concatenate.18.rows_ref, ...), custom_call_target="tpu_custom_call" | custom-call | flops 12582912000 | bytes 8388608 | tf_op jit(solution)/shard_map/near_grads/pallas_call | solution.py:456
  87.6 0.8 copy-done.2
  88.4 1.4 add_bitcast_fusion.1
  90.3 0.4 copy-done.7
  90.8 0.7 broadcast_in_dim.29.skip_ref
  91.5 1.6 collective-permute-done.6
  93.1 1.5 broadcast_select_fusion.1
  95.0 1.7 slice_bitcast_fusion
  96.7 32.4 %far_grads.1 = f32[2,1024,128]{2,1,0:T(8,128)} custom-call(bf16[2,1024,1024]{2,1,0:T(8,128)(2,1)} %x_ref.7, bf16[2,1024,1024]{2,1,0:T(8,128)(2,1)} %cot_ref.7, f32[2,8,8,24,128]{4,3,2,1,0:T(8,128)} %concatenate.18.rows_ref, f32[2,8,2,8,128]{4,3,2,1,0:T(8,128)} %reshape.535.fac_ref, bf16[2,8,8,64,512]{4,3,2,1,0:T(8,128)(2,1)} %get-tuple-element.15.loc_ref, ...), custom_call_target="tpu_custom_call" | custom-call | flops 10485760000 | bytes 16777216 | tf_op jit(solution)/shard_map/far_grads/pallas_call | solution.py:463
  129.1 40.4 %rows_out.1 = (bf16[2,1024,1024]{2,1,0:T(8,128)(2,1)}, bf16[2,1024,1024]{2,1,0:T(8,128)(2,1)}) custom-call(bf16[2,1024,1024]{2,1,0:T(8,128)(2,1)} %x_ref.7, bf16[2,1024,1024]{2,1,0:T(8,128)(2,1)} %cot_ref.7, bf16[2,1024,64]{2,1,0:T(8,128)(2,1)} %copy.135.b_ref, bf16[2,1024,64]{2,1,0:T(8,128)(2,1)} %copy.136.c_ref, ...), custom_call_target="tpu_custom_call" | custom-call | flops 25165824000 | bytes 20971520 | tf_op jit(solution)/shard_map/rows_out/pallas_call | solution.py:476
  169.5 11.9 %all-reduce.2.cloned.1.call-done = f32[2,1024,128]{2,1,0:T(8,128)} async-done(((f32[2,1024,128]{2,1,0:T(8,128)}), f32[2,1024,128]{2,1,0:T(8,128)}) %all-reduce.2.cloned.1.call-update) | async-done | bytes 1048592 | tf_op jit(solution)/shard_map/psum | solution.py:473
  181.4 1.9 fusion.28
  183.3 1.1 copy.138
  184.5 1.1 copy.137
  (76 shorter events, 4.8 us)
Async XLA Ops:
  7.2 8.5 %copy-start.6 = (s32[2,2]{1,0:T(2,128)S(1)}, s32[2,2]{1,0:T(2,128)}, u32[]{:S(2)}) copy-start(s32[2,2]{1,0:T(2,128)} %param.19) | copy-start | bytes 52
  7.2 10.7 %copy-start.4 = (bf16[2,1024,64]{1,2,0:T(8,128)(2,1)S(1)}, bf16[2,1024,64]{1,2,0:T(8,128)(2,1)}, u32[]{:S(2)}) copy-start(bf16[2,1024,64]{1,2,0:T(8,128)(2,1)} %param.14) | copy-start | bytes 786436
  7.2 11.7 %copy-start.5 = (bf16[2,1024,64]{1,2,0:T(8,128)(2,1)S(1)}, bf16[2,1024,64]{1,2,0:T(8,128)(2,1)}, u32[]{:S(2)}) copy-start(bf16[2,1024,64]{1,2,0:T(8,128)(2,1)} %param.15) | copy-start | bytes 786436
  7.2 174.2 %all-reduce.2.cloned.1.call-start = ((), (), s32[]{:S(2)}) async-start(), calls=%async_computation | async-start | bytes 2097152 | tf_op jit(solution)/shard_map/psum | solution.py:473
  11.1 46.1 %collective-permute-start.2 = (f32[2,2,8,2]{3,0,2,1:T(2,128)S(1)}, f32[2,2,8,2]{3,0,2,1:T(2,128)S(1)}, u32[]{:S(2)}, u32[]{:S(2)}) collective-permute-start(f32[2,2,8,2]{3,0,2,1:T(2,128)S(1)} %bitcast_multiply_fusion), channel_id=1, source_target_pairs={{0,1},{1,2},{2,3},{3,0},{4,5},{5,6},{6,7},{7,4},{8,9},{9,10},{10,1... | collective-permute-start | bytes 776 | tf_op jit(solution)/shard_map/ppermute | solution.py:394
  11.6 45.6 %collective-permute-start.5 = (f32[2,2,8,2]{3,0,2,1:T(2,128)S(1)}, f32[2,2,8,2]{3,0,2,1:T(2,128)S(1)}, u32[]{:S(2)}, u32[]{:S(2)}) collective-permute-start(f32[2,2,8,2]{3,0,2,1:T(2,128)S(1)} %bitcast_multiply_fusion), channel_id=1, source_target_pairs={{0,2},{1,3},{2,0},{3,1},{4,6},{5,7},{6,4},{7,5},{8,10},{9,11},{10,... | collective-permute-start | bytes 776 | tf_op jit(solution)/shard_map/ppermute | solution.py:394
  14.1 43.1 %collective-permute-start.1 = (f32[2,2,8,2]{3,0,2,1:T(2,128)S(1)}, f32[2,2,8,2]{3,0,2,1:T(2,128)S(1)}, u32[]{:S(2)}, u32[]{:S(2)}) collective-permute-start(f32[2,2,8,2]{3,0,2,1:T(2,128)S(1)} %bitcast_multiply_fusion), channel_id=1, source_target_pairs={{0,3},{1,0},{2,1},{3,2},{4,7},{5,4},{6,5},{7,6},{8,11},{9,8},{10,9... | collective-permute-start | bytes 776 | tf_op jit(solution)/shard_map/ppermute | solution.py:394
  55.3 4.6 %copy-start = (f32[2,8,64,256]{3,2,1,0:T(8,128)S(1)}, f32[2,8,64,256]{3,2,1,0:T(8,128)}, u32[]{:S(2)}) copy-start(f32[2,8,64,256]{3,2,1,0:T(8,128)} %get-tuple-element.16) | copy-start | bytes 3145732
  57.1 2.9 %collective-permute-start = (f32[2,2,8,32,256]{4,3,2,1,0:T(8,128)S(1)}, f32[2,2,8,32,256]{4,3,2,1,0:T(8,128)}, u32[]{:S(2)}, u32[]{:S(2)}) collective-permute-start(f32[2,2,8,32,256]{4,3,2,1,0:T(8,128)S(1)} %broadcast_select_fusion.5), channel_id=1, source_target_pairs={{0,1},{1,0},{2,3},{3,2},{4,5},{5,4},{6,7},{7,6},{8,9},{9,8},{10,11... | collective-permute-start | bytes 3145736 | tf_op jit(solution)/shard_map/ppermute | solution.py:285
  62.3 25.3 %copy-start.1 = (f32[2,8,32,256]{3,2,1,0:T(8,128)}, f32[2,8,32,256]{3,2,1,0:T(8,128)S(1)}, u32[]{:S(2)}) copy-start(f32[2,8,32,256]{3,2,1,0:T(8,128)S(1)} %get-tuple-element.19) | copy-start | bytes 1572868
  62.3 25.3 %collective-permute-start.3 = (f32[2,8,32,256]{3,2,1,0:T(8,128)S(1)}, f32[2,8,32,256]{3,2,1,0:T(8,128)S(1)}, u32[]{:S(2)}, u32[]{:S(2)}) collective-permute-start(f32[2,8,32,256]{3,2,1,0:T(8,128)S(1)} %get-tuple-element.18), channel_id=1, source_target_pairs={{0,2},{1,3},{2,0},{3,1},{4,6},{5,7},{6,4},{7,5},{8,10},{9,11},{10,... | collective-permute-start | bytes 1572872 | tf_op jit(solution)/shard_map/ppermute | solution.py:304
  62.7 25.7 %collective-permute-start.4 = (f32[2,8,32,256]{3,2,1,0:T(8,128)S(1)}, f32[2,8,32,256]{3,2,1,0:T(8,128)}, u32[]{:S(2)}, u32[]{:S(2)}) collective-permute-start(f32[2,8,32,256]{3,2,1,0:T(8,128)S(1)} %get-tuple-element.19), channel_id=1, source_target_pairs={{0,2},{1,3},{2,0},{3,1},{4,6},{5,7},{6,4},{7,5},{8,10},{9,11},{10,... | collective-permute-start | bytes 1572872 | tf_op jit(solution)/shard_map/ppermute | solution.py:305
  87.6 0.8 copy-start.2
  88.4 1.4 copy-start.3
  90.0 0.7 copy-start.7
  90.2 2.9 %collective-permute-start.6 = (f32[2,2,8,32,256]{4,3,2,1,0:T(8,128)S(1)}, f32[2,2,8,32,256]{4,3,2,1,0:T(8,128)}, u32[]{:S(2)}, u32[]{:S(2)}) collective-permute-start(f32[2,2,8,32,256]{4,3,2,1,0:T(8,128)S(1)} %fusion.1), channel_id=1, source_target_pairs={{0,1},{1,0},{2,3},{3,2},{4,5},{5,4},{6,7},{7,6},{8,9},{9,8},{10,11... | collective-permute-start | bytes 3145736 | tf_op jit(solution)/shard_map/ppermute | solution.py:324
Sparse Core Ops, SparseCore 0:
  129.2 52.1 all-reduce.1
